TPU v7x, 128 devices: a whole 4x4x4 slice. The times are simulated.
128 devices in a mesh: section: 2 (over y_lo), dp: 64 (over y_hi, z, x, core).
Axes of the slice: x: 4, y: 4 (y_hi: 2, y_lo: 2; y = y_hi * 2 + y_lo), z: 4, core: 2. Of those that a mesh axis runs over, the one named last changes fastest.
Arguments:
- tokens: bfloat16 [2, 8192, 1024], P(None, 'dp'), may hold values from -6 to 6
- positions: int32 [2, 8192], P(None, 'dp'), may hold values from 0 to 127, as said below
- cotangent: bfloat16 [2, 8192, 1024], P(None, 'dp'), may hold values from -16 to 16
- w_qkv: bfloat16 [2, 1024, 3072], P('section', 'dp'), may hold values from -0.1875 to 0.1875
- b_query: bfloat16 [2, 1024], P('section', 'dp'), may hold values from -3 to 3
- b_value: bfloat16 [2, 1024], P('section', 'dp'), may hold values from -3 to 3
- w_out: bfloat16 [2, 1024, 1024], P('section', 'dp'), may hold values from -0.75 to 0.75
- b_out: bfloat16 [2, 1024], P('section', 'dp'), may hold values from -3 to 3
- w_up: bfloat16 [2, 1024, 4096], P('section', 'dp'), may hold values from -0.1875 to 0.1875
- b_up: bfloat16 [2, 4096], P('section', 'dp'), may hold values from -3 to 3
- w_down: bfloat16 [2, 4096, 1024], P('section', 'dp'), may hold values from -0.09375 to 0.09375
- b_down: bfloat16 [2, 1024], P('section', 'dp'), may hold values from -3 to 3
- gain_one: bfloat16 [2, 1024], P('section', 'dp'), may hold values from 0.5 to 1.5
- shift_one: bfloat16 [2, 1024], P('section', 'dp'), may hold values from -2 to 2
- gain_two: bfloat16 [2, 1024], P('section', 'dp'), may hold values from 0.5 to 1.5
- shift_two: bfloat16 [2, 1024], P('section', 'dp'), may hold values from -2 to 2
Outputs:
- layer_out: bfloat16 [2, 2, 8192, 1024], P('section', None, 'dp')
- input_grad: bfloat16 [2, 2, 8192, 1024], P('section', None, 'dp')
- grad_w_qkv: float32 [2, 1024, 3072], P('section', 'dp')
- grad_b_query: float32 [2, 1024], P('section', 'dp')
- grad_b_value: float32 [2, 1024], P('section', 'dp')
- grad_w_out: float32 [2, 1024, 1024], P('section', 'dp')
- grad_b_out: float32 [2, 1024], P('section', 'dp')
- grad_w_up: float32 [2, 1024, 4096], P('section', 'dp')
- grad_b_up: float32 [2, 4096], P('section', 'dp')
- grad_w_down: float32 [2, 4096, 1024], P('section', 'dp')
- grad_b_down: float32 [2, 1024], P('section', 'dp')
- grad_gain_one: float32 [2, 1024], P('section', 'dp')
- grad_shift_one: float32 [2, 1024], P('section', 'dp')
- grad_gain_two: float32 [2, 1024], P('section', 'dp')
- grad_shift_two: float32 [2, 1024], P('section', 'dp')
Inputs may be any that keep to these rules, and one draw needn't show every extreme that they name: positions counts up by one along each sequence from 0; a sequence lies within one block of 128 rows of one device and micro-batch, each block begins a sequence, and some sequence is 128 long.
All inputs are finite; a program needn't handle non-finite values.
Results may differ from a plain program's by a relative error of at most 0.015.
Values may be sent and summed in bfloat16 or wider, within the bound.
A program may use at most 320 MiB of HBM per device.

v0:
```python
from functools import partial
import math

import jax
import jax.numpy as jnp
from jax import lax
from jax.sharding import Mesh
from jax.sharding import PartitionSpec as P

HEADS = 16
HEAD = 64
DP = ("dp_0", "dp_1", "dp_2", "dp_3")


epsilon = 1e-05
masked_value = -1000000000.0


def side_by_side(arrays, axis, dim, along):
    widths = [math.prod(a.shape[along:]) for a in arrays]
    both = jnp.concatenate(
        [a.reshape(*a.shape[:along], w) for a, w in zip(arrays, widths)], axis=along
    )
    out = lax.all_gather(both, axis, axis=dim, tiled=True)
    pieces = jnp.split(out, [sum(widths[:k]) for k in range(1, len(widths))], axis=along)
    return tuple((b.reshape(*out.shape[:along], *a.shape[along:]) for a, b in zip(arrays, pieces)))


def in_one_piece(arrays, axis, dim, along):
    ends, at = ([], 0)
    for a in arrays[:-1]:
        at += a.shape[along]
        ends.append(at)
    both = jnp.concatenate(arrays, axis=along)
    return tuple(jnp.split(lax.all_gather(both, axis, axis=dim, tiled=True), ends, axis=along))


def from_behind(block, axis, distance):
    devices = range(lax.axis_size(axis))
    route = [(i - distance, i) for i in devices if i - distance in devices]
    return lax.ppermute(block, axis, route)


def split_up(x, dim, length):
    before, after = (x.shape[:dim], x.shape[dim + 1 :])
    return jnp.moveaxis(x.reshape(*before, length, -1, *after), dim, 0)


def scatter_pairs(x, chips, core, dim):
    sizes = (lax.axis_size(chips), lax.axis_size(core))
    pieces = split_up(x, dim, sizes[0] * sizes[1])
    inside = pieces.shape[1:]
    pieces = pieces.reshape(*sizes, *inside).swapaxes(0, 1).reshape(-1, *inside)
    pieces = lax.psum_scatter(pieces, core, scatter_dimension=0, tiled=True)
    return lax.psum_scatter(pieces, chips, scatter_dimension=0, tiled=True)[0]


def norm_rows(values, gain, shift):
    center = values - jnp.mean(values, axis=-1, keepdims=True)
    spread = jnp.mean(center * center, axis=-1, keepdims=True)
    return center * lax.rsqrt(spread + epsilon) * gain + shift


def attention_bias(token_places, row_count):
    query_index = jnp.arange(row_count, dtype=jnp.int32)[:, None]
    key_index = jnp.arange(row_count, dtype=jnp.int32)[None, :]
    distance = query_index - key_index
    allowed = (distance >= 0) & (distance <= token_places[:, None])
    slopes = 2.0 ** (-8.0 * jnp.arange(1, HEADS + 1, dtype=jnp.float32) / HEADS)
    bias_table = -slopes[:, None, None] * distance.astype(jnp.float32)[None]
    return (bias_table, allowed)


def head_scores(queries, keys_all, bias_table, allowed, row_count):
    scores = jnp.einsum(
        "qhd,khd->hqk",
        queries.reshape(row_count, HEADS, HEAD),
        keys_all.reshape(row_count, HEADS, HEAD),
        preferred_element_type=jnp.float32,
    )
    scores = scores * HEAD ** (-0.5) + bias_table
    return jnp.where(allowed[None], scores, masked_value)


def forward_layer(inbound, token_places, weights):
    (
        w_qkv,
        b_query,
        b_value,
        w_out,
        b_out,
        w_up,
        b_up,
        w_down,
        b_down,
        gain_one,
        shift_one,
        gain_two,
        shift_two,
    ) = weights
    row_count, model_width = inbound.shape
    hidden_in = inbound.astype(jnp.float32)
    normed = norm_rows(
        hidden_in, gain_one.astype(jnp.float32), shift_one.astype(jnp.float32)
    ).astype(jnp.bfloat16)
    mixed_proj = jnp.dot(normed, w_qkv, preferred_element_type=jnp.float32)
    queries = (mixed_proj[:, :model_width] + b_query.astype(jnp.float32)).astype(jnp.bfloat16)
    keys_all = mixed_proj[:, model_width : 2 * model_width].astype(jnp.bfloat16)
    values_all = (mixed_proj[:, 2 * model_width :] + b_value.astype(jnp.float32)).astype(
        jnp.bfloat16
    )
    bias_table, allowed = attention_bias(token_places, row_count)
    masked = head_scores(queries, keys_all, bias_table, allowed, row_count)
    row_max = jnp.max(masked, axis=-1, keepdims=True)
    row_total = jnp.sum(jnp.exp(masked - row_max), axis=-1, keepdims=True)
    log_total = row_max + jnp.log(row_total)
    softmax_probs = jnp.exp(masked - log_total).astype(jnp.bfloat16)
    attended = jnp.einsum(
        "hqk,khd->qhd",
        softmax_probs,
        values_all.reshape(row_count, HEADS, HEAD),
        preferred_element_type=jnp.float32,
    )
    attended = attended.reshape(row_count, model_width).astype(jnp.bfloat16)
    middle = (
        hidden_in
        + jnp.dot(attended, w_out, preferred_element_type=jnp.float32)
        + b_out.astype(jnp.float32)
    )
    normed_two = norm_rows(
        middle, gain_two.astype(jnp.float32), shift_two.astype(jnp.float32)
    ).astype(jnp.bfloat16)
    upward = jnp.dot(normed_two, w_up, preferred_element_type=jnp.float32) + b_up.astype(
        jnp.float32
    )
    activated = jax.nn.gelu(upward, approximate=True).astype(jnp.bfloat16)
    result = (
        middle
        + jnp.dot(activated, w_down, preferred_element_type=jnp.float32)
        + b_down.astype(jnp.float32)
    )
    kept_values = (
        hidden_in,
        normed,
        queries,
        keys_all,
        values_all,
        log_total,
        attended,
        middle,
        normed_two,
        upward,
        activated,
    )
    return (result, kept_values)


def backward_layer(upstream, token_places, weights, kept_values):
    (
        w_qkv,
        b_query,
        b_value,
        w_out,
        b_out,
        w_up,
        b_up,
        w_down,
        b_down,
        gain_one,
        shift_one,
        gain_two,
        shift_two,
    ) = weights
    (
        hidden_in,
        normed,
        queries,
        keys_all,
        values_all,
        log_total,
        attended,
        middle,
        normed_two,
        upward,
        activated,
    ) = kept_values
    row_count, model_width = upstream.shape
    grad_result = upstream.astype(jnp.float32)
    grad_b_down = jnp.sum(grad_result, axis=0)
    grad_w_down = jnp.dot(activated.T, upstream, preferred_element_type=jnp.float32)
    grad_act = jnp.dot(upstream, w_down.T, preferred_element_type=jnp.float32)
    gelu_value, gelu_back = jax.vjp(partial(jax.nn.gelu, approximate=True), upward)
    grad_upward = gelu_back(grad_act)[0].astype(jnp.bfloat16)
    grad_b_up = jnp.sum(grad_upward.astype(jnp.float32), axis=0)
    grad_w_up = jnp.dot(normed_two.T, grad_upward, preferred_element_type=jnp.float32)
    grad_normed_two = jnp.dot(grad_upward, w_up.T, preferred_element_type=jnp.float32)
    norm_value, norm_back = jax.vjp(
        norm_rows, middle, gain_two.astype(jnp.float32), shift_two.astype(jnp.float32)
    )
    grad_middle_part, grad_gain_two, grad_shift_two = norm_back(grad_normed_two)
    grad_middle = grad_result + grad_middle_part
    grad_branch = grad_middle.astype(jnp.bfloat16)
    grad_b_out = jnp.sum(grad_branch.astype(jnp.float32), axis=0)
    grad_w_out = jnp.dot(attended.T, grad_branch, preferred_element_type=jnp.float32)
    grad_attended = jnp.dot(grad_branch, w_out.T, preferred_element_type=jnp.float32).astype(
        jnp.bfloat16
    )
    grad_heads = grad_attended.reshape(row_count, HEADS, HEAD)
    bias_table, allowed = attention_bias(token_places, row_count)
    masked = head_scores(queries, keys_all, bias_table, allowed, row_count)
    float_probs = jnp.exp(masked - log_total)
    softmax_probs = float_probs.astype(jnp.bfloat16)
    grad_values = jnp.einsum(
        "hqk,qhd->khd", softmax_probs, grad_heads, preferred_element_type=jnp.float32
    )
    grad_probs = jnp.einsum(
        "qhd,khd->hqk",
        grad_heads,
        values_all.reshape(row_count, HEADS, HEAD),
        preferred_element_type=jnp.float32,
    )
    row_delta = jnp.sum(float_probs * grad_probs, axis=-1, keepdims=True)
    grad_scores = (float_probs * (grad_probs - row_delta)).astype(jnp.bfloat16)
    grad_queries = jnp.einsum(
        "hqk,khd->qhd",
        grad_scores,
        keys_all.reshape(row_count, HEADS, HEAD),
        preferred_element_type=jnp.float32,
    ) * HEAD ** (-0.5)
    grad_keys = jnp.einsum(
        "hqk,qhd->khd",
        grad_scores,
        queries.reshape(row_count, HEADS, HEAD),
        preferred_element_type=jnp.float32,
    ) * HEAD ** (-0.5)
    grad_queries = grad_queries.reshape(row_count, model_width).astype(jnp.bfloat16)
    grad_keys = grad_keys.reshape(row_count, model_width).astype(jnp.bfloat16)
    grad_values = grad_values.reshape(row_count, model_width).astype(jnp.bfloat16)
    grad_mixed = jnp.concatenate([grad_queries, grad_keys, grad_values], axis=1)
    grad_b_query = jnp.sum(grad_queries.astype(jnp.float32), axis=0)
    grad_b_value = jnp.sum(grad_values.astype(jnp.float32), axis=0)
    grad_w_qkv = jnp.dot(normed.T, grad_mixed, preferred_element_type=jnp.float32)
    grad_normed = jnp.dot(grad_mixed, w_qkv.T, preferred_element_type=jnp.float32)
    first_value, first_back = jax.vjp(
        norm_rows, hidden_in, gain_one.astype(jnp.float32), shift_one.astype(jnp.float32)
    )
    grad_hidden_part, grad_gain_one, grad_shift_one = first_back(grad_normed)
    grad_input = grad_middle + grad_hidden_part
    weight_grads = (
        grad_w_qkv,
        grad_b_query,
        grad_b_value,
        grad_w_out,
        grad_b_out,
        grad_w_up,
        grad_b_up,
        grad_w_down,
        grad_b_down,
        grad_gain_one,
        grad_shift_one,
        grad_gain_two,
        grad_shift_two,
    )
    return (grad_input, weight_grads)


def body(
    tokens,
    positions,
    cotangent,
    w_qkv,
    b_query,
    b_value,
    w_out,
    b_out,
    w_up,
    b_up,
    w_down,
    b_down,
    gain_one,
    shift_one,
    gain_two,
    shift_two,
):
    shards = (
        w_qkv,
        b_query,
        b_value,
        w_out,
        b_out,
        w_up,
        b_up,
        w_down,
        b_down,
        gain_one,
        shift_one,
        gain_two,
        shift_two,
    )
    gathered = (
        *side_by_side((w_qkv, b_query, b_value, w_out, b_out, w_up), DP, 1, 2),
        *side_by_side((b_up, w_down), DP, 1, 2),
        *in_one_piece((b_down, gain_one, shift_one, gain_two, shift_two), DP, 1, 0),
    )
    weights = tuple((piece[0] for piece in gathered))
    section_index = lax.axis_index("section")
    micro_count, row_count, model_width = tokens.shape
    empty_rows = jnp.zeros((row_count, model_width), jnp.bfloat16)
    out_slots = [empty_rows for slot_index in range(micro_count)]
    kept_ticks = []
    received = empty_rows
    for tick_index in range(micro_count + 1):
        batch_index = jnp.clip(tick_index - section_index, 0, micro_count - 1)
        inbound = jnp.where(section_index == 0, tokens[min(tick_index, micro_count - 1)], received)
        token_places = lax.dynamic_index_in_dim(positions, batch_index, 0, keepdims=False)
        result, kept_values = forward_layer(inbound, token_places, weights)
        result_low = result.astype(jnp.bfloat16)
        for slot_index in range(micro_count):
            out_slots[slot_index] = jnp.where(
                tick_index - section_index == slot_index, result_low, out_slots[slot_index]
            )
        kept_ticks.append(kept_values)
        if tick_index < micro_count:
            received = from_behind(result_low, "section", 1)
    grad_slots = [empty_rows for slot_index in range(micro_count)]
    totals = [jnp.zeros(piece.shape, jnp.float32) for piece in weights]
    owned = [jnp.zeros(piece.shape, jnp.float32) for piece in shards]
    arriving = empty_rows
    for tick_index in range(micro_count + 1):
        signed_index = micro_count - tick_index - section_index
        is_valid = (signed_index >= 0) & (signed_index < micro_count)
        batch_index = jnp.clip(signed_index, 0, micro_count - 1)
        outer_grad = lax.dynamic_index_in_dim(cotangent, batch_index, 0, keepdims=False)
        upstream = jnp.where(section_index == 1, outer_grad, arriving)
        upstream = jnp.where(is_valid, upstream, empty_rows)
        token_places = lax.dynamic_index_in_dim(positions, batch_index, 0, keepdims=False)
        grad_input, weight_grads = backward_layer(
            upstream, token_places, weights, kept_ticks[micro_count - tick_index]
        )
        grad_low = grad_input.astype(jnp.bfloat16)
        for slot_index in range(micro_count):
            grad_slots[slot_index] = jnp.where(
                signed_index == slot_index, grad_low, grad_slots[slot_index]
            )
        totals = [total + grad for total, grad in zip(totals, weight_grads)]
        if tick_index < micro_count:
            arriving = from_behind(grad_low, "section", -1)
    owned = jax.tree.map(
        lambda part: scatter_pairs(part, ("dp_0", "dp_1", "dp_2"), "dp_3", 1),
        tuple((total[None] for total in totals)),
    )
    layer_out = jnp.stack(out_slots)[None]
    input_grad = jnp.stack(grad_slots)[None]
    return (
        layer_out,
        input_grad,
        owned[0],
        owned[1],
        owned[2],
        owned[3],
        owned[4],
        owned[5],
        owned[6],
        owned[7],
        owned[8],
        owned[9],
        owned[10],
        owned[11],
        owned[12],
    )


def solution(mesh):
    torus = Mesh(
        mesh.devices.reshape(mesh.shape["section"], 2, 4, 4, 2),
        ("section", "dp_0", "dp_1", "dp_2", "dp_3"),
    )
    placed = (
        P(None, DP, None),
        P(None, DP),
        P(None, DP, None),
        P("section", DP, None),
        P("section", DP),
        P("section", DP),
        P("section", DP, None),
        P("section", DP),
        P("section", DP, None),
        P("section", DP),
        P("section", DP, None),
        P("section", DP),
        P("section", DP),
        P("section", DP),
        P("section", DP),
        P("section", DP),
    )
    return jax.shard_map(
        body,
        mesh=torus,
        in_specs=placed,
        out_specs=(
            P("section", None, DP, None),
            P("section", None, DP, None),
            P("section", DP, None),
            P("section", DP),
            P("section", DP),
            P("section", DP, None),
            P("section", DP),
            P("section", DP, None),
            P("section", DP),
            P("section", DP, None),
            P("section", DP),
            P("section", DP),
            P("section", DP),
            P("section", DP),
            P("section", DP),
        ),
        check_vma=False,
    )
```

profile of v0, /device:TPU:0, one launch (start us, length us, event | category | flops | bytes accessed | tf_op | source)
XLA Modules:
  0.0 1543.6 jit_solution(16129246060293317926)
XLA Ops:
  14.7 98.2 %all-gather = bf16[64,16,5]{1,2,0:T(8,128)(2,1)S(1)} all-gather(bf16[1,16,5]{1,2,0:T(8,128)(2,1)S(1)} %bitcast.499), channel_id=1, replica_groups=mesh['section'=2,'dp_0'=2,'dp_1'=4,'dp_2'=4,'dp_3'=2] {'dp_0','dp_1','dp..., dimensions={0}, use_global_device_ids=true | all-gather | bytes 10400 | tf_op jit(solution)/shard_map/all_gather | solution.py:35
  116.9 90.4 %all-gather.4.cloned.1.call-done = bf16[1,1024,8195]{2,1,0:T(8,128)(2,1)} async-done(((bf16[1,16,8195]{2,1,0:T(8,128)(2,1)}), bf16[1,1024,8195]{2,1,0:T(8,128)(2,1)}) %all-gather.4.cloned.1.call-update) | async-done | bytes 16783376 | tf_op jit(solution)/shard_map/all_gather | solution.py:24
  207.3 3.9 fusion.14
  218.0 6.4 convolution_add_fusion.2
  231.5 5.0 collective-permute-done
  236.9 3.9 fusion.13
  252.7 6.4 convolution_add_fusion.1
  259.2 4.2 fusion.49
  263.5 4.4 collective-permute-start.1
  267.9 5.5 collective-permute-done.1
  274.7 3.9 fusion.12
  286.5 6.5 convolution_add_fusion
  293.1 5.6 convert_reduce_fusion.3
  298.7 8.2 multiply_reduce_fusion.5
  320.2 5.8 fusion.174
  332.2 4.4 collective-permute-done.2
  337.4 9.2 convert_reduce_fusion.2
  360.3 5.5 fusion.173
  368.9 6.2 collective-permute-done.3
  375.3 8.5 convert_reduce_fusion.1
  383.9 7.5 multiply_reduce_fusion.3
  396.6 8.3 fusion.108
  404.9 6.5 fusion.107
  418.3 13.5 add_add_fusion.2
  431.9 10.7 copy.221
  443.7 12.1 fusion.171
  455.7 10.5 fusion.170
  466.2 18.5 %add_add_fusion.1 = f32[1024,4096]{1,0:T(8,128)} fusion(f32[1024,4096]{1,0:T(8,128)} %fusion.171, f32[1024,4096]{1,0:T(8,128)} %fusion.170, bf16[128,4096]{1,0:T(8,128)(2,1)} %copy-done.51, f32[128,1024]{1,0:T(8,128)S(1)} %copy-done.12, f32[1024]{0:T(1024)S(1)} %bitcast.459, f32[1024]{0:T(1024)S(1)} %bitcast.453, f32[128]{0:T(128)S(1)} %copy-done.110, ...), kind=kOutput, calls=%fused_computation.1 | convolution fusion | flops 1082785792 | bytes 51913728 | tf_op jit(solution)/shard_map/dot_general | solution.py:195
  484.7 11.6 copy.229
  497.3 12.0 fusion.112
  509.3 12.4 fusion.172
  521.8 19.5 %add_add_fusion = f32[4096,1024]{1,0:T(8,128)} fusion(f32[4096,1024]{1,0:T(8,128)} %fusion.112, f32[4096,1024]{1,0:T(8,128)} %fusion.172, bf16[128,1024]{1,0:T(8,128)(2,1)S(1)} %copy-done.16, f32[128,4096]{1,0:T(8,128)} %copy-done.40), kind=kOutput, calls=%fused_computation | convolution fusion | flops 1086849024 | bytes 52690944 | tf_op jit(solution)/shard_map/dot_general | solution.py:190
  541.3 11.8 copy.231
  555.6 5.1 fusion.175
  568.7 12.8 reduce-scatter.49.cloned.1.call-done
  582.8 7.7 select_bitcast_fusion.3
  595.3 13.9 reduce-scatter.55.cloned.1.call-done
  609.1 13.9 reduce-scatter.57.cloned.1.call-done
  623.0 13.7 reduce-scatter.59.cloned.1.call-done
  636.7 13.9 reduce-scatter.61.cloned.1.call-done
  650.6 13.7 reduce-scatter.63.cloned.1.call-done
  664.4 13.9 reduce-scatter.65.cloned.1.call-done
  678.2 13.7 reduce-scatter.67.cloned.1.call-done
  692.0 13.7 reduce-scatter.47.cloned.1.call-done
  705.7 186.2 %all-reduce.9 = (f32[32,1,16]{2,1,0:T(1,128)S(1)}, f32[32,1,16]{2,1,0:T(1,128)S(1)}, f32[32,1,16]{2,1,0:T(1,128)S(1)}, f32[32,1,64]{2,0,1:T(8,128)S(1)}, f32[32,...) all-reduce(f32[32,1,16]{2,1,0:T(1,128)} %bitcast.491, ...), channel_id=5, replica_groups=mesh['section'=2,'dp_0'=2,'dp_1'=4,'dp_2'=4,'dp_3'=2] {'dp_0','dp_1','dp..., use_global_device_ids=true, to_apply=%region_39.40.clone | all-reduce | flops 6144 | bytes 49152
  901.6 231.1 %reduce-scatter.37.cloned.1.call-done = f32[1,1,16,3072]{3,2,1,0:T(8,128)} async-done(((f32[32,1,16,3072]{3,2,1,0:T(8,128)}), f32[1,1,16,3072]{3,2,1,0:T(8,128)}) %reduce-scatter.37.cloned.1.call-update) | async-done | bytes 196624 | tf_op jit(solution)/shard_map/reduce_scatter | solution.py:55
  1132.8 202.5 %reduce-scatter.45.cloned.1.call-done = f32[1,1,16,4096]{3,2,1,0:T(8,128)} async-done(((f32[32,1,16,4096]{3,2,1,0:T(8,128)}), f32[1,1,16,4096]{3,2,1,0:T(8,128)}) %reduce-scatter.45.cloned.1.call-update) | async-done | bytes 262160 | tf_op jit(solution)/shard_map/reduce_scatter | solution.py:55
  1335.2 201.3 %reduce-scatter.51.cloned.1.call-done = f32[1,1,64,1024]{3,2,1,0:T(8,128)} async-done(((f32[32,1,64,1024]{3,2,1,0:T(8,128)}), f32[1,1,64,1024]{3,2,1,0:T(8,128)}) %reduce-scatter.51.cloned.1.call-update) | async-done | bytes 262160 | tf_op jit(solution)/shard_map/reduce_scatter | solution.py:55
  (496 shorter events, 122.7 us)
Async XLA Ops:
  7.2 107.8 %copy-start.9 = (bf16[2,128,1024]{2,1,0:T(8,128)(2,1)S(1)}, bf16[2,128,1024]{2,1,0:T(8,128)(2,1)}, u32[]{:S(2)}) copy-start(bf16[2,128,1024]{2,1,0:T(8,128)(2,1)} %param.16) | copy-start | bytes 1572868
  7.2 108.1 %all-gather.6.cloned.1.call-start = ((), (), s32[]{:S(2)}) async-start(), calls=%async_computation.18 | async-start | bytes 9584640 | tf_op jit(solution)/shard_map/all_gather | solution.py:24
  9.7 197.5 %all-gather.4.cloned.1.call-start = ((), (), s32[]{:S(2)}) async-start(), calls=%async_computation.17 | async-start | bytes 17305600 | tf_op jit(solution)/shard_map/all_gather | solution.py:24
  13.9 552.7 %reduce-scatter.39.cloned.1.call-start = ((), (), s32[]{:S(2)}) async-start(), calls=%async_computation.21 | async-start | bytes 6291456 | tf_op jit(solution)/shard_map/reduce_scatter | solution.py:54
  113.1 100.4 %copy-start.125 = (f32[16]{0:T(128)}, f32[16]{0:T(128)S(1)}, u32[]{:S(2)}) copy-start(f32[16]{0:T(128)S(1)} %power_negate_fusion) | copy-start | bytes 196
  115.0 96.2 %copy-start.95 = (f32[128]{0:T(128)}, f32[128]{0:T(128)S(1)}, u32[]{:S(2)}) copy-start(f32[128]{0:T(128)S(1)} %broadcast_multiply_fusion.5) | copy-start | bytes 1540
  115.2 96.0 %copy-start.113 = (f32[128]{0:T(128)}, f32[128]{0:T(128)S(1)}, u32[]{:S(2)}) copy-start(f32[128]{0:T(128)S(1)} %fusion.88) | copy-start | bytes 1540
  115.2 96.0 %copy-start.101 = (f32[128]{0:T(128)}, f32[128]{0:T(128)S(1)}, u32[]{:S(2)}) copy-start(f32[128]{0:T(128)S(1)} %fusion.151) | copy-start | bytes 1540
  115.3 109.1 %copy-start.103 = (f32[1,1024]{1,0:T(1,128)}, f32[1,1024]{1,0:T(1,128)S(1)}, u32[]{:S(2)}) copy-start(f32[1,1024]{1,0:T(1,128)S(1)} %get-tuple-element.81) | copy-start | bytes 12292
  213.5 11.0 slice-start.5
  214.4 10.0 copy-start.56
  214.4 10.0 slice-start.6
  228.0 8.5 collective-permute-start
  246.6 12.6 slice-start.8
  248.6 10.6 slice-start.9
  263.5 9.9 collective-permute-start.1
  281.3 11.7 slice-start.11
  286.3 20.6 %copy-start.5 = (f32[128,1024]{1,0:T(8,128)}, f32[128,1024]{1,0:T(8,128)S(1)}, u32[]{:S(2)}) copy-start(f32[128,1024]{1,0:T(8,128)S(1)} %get-tuple-element.99) | copy-start | bytes 1572868
  327.9 8.8 collective-permute-start.2
  329.5 17.1 %slice-start = ((s8[17039360]{0:T(1024)(128)(4,1)}), s8[4194304]{0:T(1024)(128)(4,1)S(1)}, s32[]{:S(2)}) async-start(s8[17039360]{0:T(1024)(128)(4,1)} %bitcast.393), calls=%async_computation.36 | async-start | bytes 8388608
  337.4 13.5 copy-start.17
  366.6 8.5 collective-permute-start.3
  375.3 16.5 %copy-start.15 = (bf16[128,1024]{1,0:T(8,128)(2,1)}, bf16[128,1024]{1,0:T(8,128)(2,1)S(1)}, u32[]{:S(2)}) copy-start(bf16[128,1024]{1,0:T(8,128)(2,1)S(1)} %get-tuple-element.51) | copy-start | bytes 786436
  395.6 171.7 %reduce-scatter.35.cloned.1.call-start = ((), (), s32[]{:S(2)}) async-start(), calls=%async_computation.19 | async-start | bytes 18874368 | tf_op jit(solution)/shard_map/reduce_scatter | solution.py:54
  417.3 14.5 copy-start.44
  417.7 14.2 copy-start.46
  418.3 13.6 copy-start.42
  442.6 125.2 %reduce-scatter.43.cloned.1.call-start = ((), (), s32[]{:S(2)}) async-start(), calls=%async_computation.23 | async-start | bytes 25165824 | tf_op jit(solution)/shard_map/reduce_scatter | solution.py:54
  443.7 12.1 copy-start.50
  496.3 13.1 copy-start.19
  496.3 85.2 %reduce-scatter.49.cloned.1.call-start = ((), (), s32[]{:S(2)}) async-start(), calls=%async_computation.26 | async-start | bytes 25165824 | tf_op jit(solution)/shard_map/reduce_scatter | solution.py:54
  497.3 12.1 copy-start.27
  509.3 12.4 copy-start.16
  553.2 42.1 %reduce-scatter.53.cloned.1.call-start = ((), (), s32[]{:S(2)}) async-start(), calls=%async_computation.28 | async-start | bytes 49152
  554.6 54.6 %reduce-scatter.55.cloned.1.call-start = ((), (), s32[]{:S(2)}) async-start(), calls=%async_computation.29 | async-start | bytes 49152
  555.4 67.7 %reduce-scatter.57.cloned.1.call-start = ((), (), s32[]{:S(2)}) async-start(), calls=%async_computation.30 | async-start | bytes 49152
  555.5 10.3 copy-start.85
  555.5 10.3 copy-start.86
  561.4 75.3 %reduce-scatter.59.cloned.1.call-start = ((), (), s32[]{:S(2)}) async-start(), calls=%async_computation.31 | async-start | bytes 49152
  562.6 88.1 %reduce-scatter.61.cloned.1.call-start = ((), (), s32[]{:S(2)}) async-start(), calls=%async_computation.32 | async-start | bytes 49152
  563.4 101.0 %reduce-scatter.63.cloned.1.call-start = ((), (), s32[]{:S(2)}) async-start(), calls=%async_computation.33 | async-start | bytes 49152
  564.2 114.1 %reduce-scatter.65.cloned.1.call-start = ((), (), s32[]{:S(2)}) async-start(), calls=%async_computation.34 | async-start | bytes 49152
  565.0 127.0 %reduce-scatter.67.cloned.1.call-start = ((), (), s32[]{:S(2)}) async-start(), calls=%async_computation.35 | async-start | bytes 49152
  565.8 139.9 %reduce-scatter.47.cloned.1.call-start = ((), (), s32[]{:S(2)}) async-start(), calls=%async_computation.25 | async-start | bytes 49152 | tf_op jit(solution)/shard_map/reduce_scatter | solution.py:54
  566.6 335.0 %reduce-scatter.41.cloned.1.call-start = ((), (), s32[]{:S(2)}) async-start(), calls=%async_computation.22 | async-start | bytes 2162688 | tf_op jit(solution)/shard_map/reduce_scatter | solution.py:55
  567.2 565.6 %reduce-scatter.37.cloned.1.call-start = ((), (), s32[]{:S(2)}) async-start(), calls=%async_computation.20 | async-start | bytes 6488064 | tf_op jit(solution)/shard_map/reduce_scatter | solution.py:55
  567.8 767.5 %reduce-scatter.45.cloned.1.call-start = ((), (), s32[]{:S(2)}) async-start(), calls=%async_computation.24 | async-start | bytes 8650752 | tf_op jit(solution)/shard_map/reduce_scatter | solution.py:55
  568.3 968.2 %reduce-scatter.51.cloned.1.call-start = ((), (), s32[]{:S(2)}) async-start(), calls=%async_computation.27 | async-start | bytes 8650752 | tf_op jit(solution)/shard_map/reduce_scatter | solution.py:55
  (117 other events, 532.0 us)
Sparse Core Ops, SparseCore 0:
  11.9 87.3 all-gather.5
  103.0 104.2 all-gather.3
  395.7 13.2 reduce-scatter.38
  442.8 22.9 reduce-scatter.34
  496.4 28.1 reduce-scatter.42
  553.3 28.1 reduce-scatter.48
  583.9 11.2 reduce-scatter.52
  597.7 11.4 reduce-scatter.54
  611.5 11.4 reduce-scatter.56
  625.3 11.4 reduce-scatter.58
  639.1 11.4 reduce-scatter.60
  652.9 11.4 reduce-scatter.62
  666.8 11.4 reduce-scatter.64
  680.5 11.4 reduce-scatter.66
  694.2 11.4 reduce-scatter.46
  708.6 189.0 reduce-scatter.40
  903.3 229.3 reduce-scatter.36
  1135.6 199.5 reduce-scatter.44
  1338.2 198.3 reduce-scatter.50
where the time goes:
time: 1550 us; the launch traced here: 1540 us
  waiting for transfers between devices  874 us (56%)
  blocking collectives  284 us (18%)
  matrix products  256 us (17%)
  local copies, waits for them, and re-layouts  82.4 us (5%)
  other arithmetic  18.2 us (1%)
  between operations  16.8 us (1%)
    reduce_scatter x4, waiting for transfers between devices, scatter_pairs(): return lax.psum_scatter(pieces, chips, scatter_dimension=0, tiled=True)[0]  635 us
    unnamed x1, blocking collectives  186 us
    unnamed x27, waiting for transfers between devices  101 us
    all_gather x1, blocking collectives, in_one_piece(): lax.all_gather(both, axis, axis=dim, tiled=True)  98.2 us
    all_gather x2, waiting for transfers between devices, side_by_side(): out = lax.all_gather(both, axis, axis=dim, tiled=True)  90.4 us
    dot_general x3, matrix products, backward_layer(): jnp.dot(activated.T, upstream, preferred_element_type=jnp.float32)  44 us
    dot_general x3, matrix products, backward_layer(): jnp.dot(normed_two.T, grad_upward, preferred_element_type=jnp.float32)  41 us
    transpose x5, local copies, waits for them, and re-layouts, scatter_pairs(): pieces = pieces.reshape(*sizes, *inside).swapaxes(0, 1).reshape(-1, *inside)  37 us
  transfers between devices with their start and end apart: 23, of which 18 were waited for; matrix products, arithmetic and copies ran while one was open for 13% of the time, Pallas kernels for 0%

commit v1 on v0

v1 whole, which is shorter than its diff:
```python
from functools import partial

import jax
import jax.numpy as jnp
from jax import lax
from jax.experimental import pallas as pl
from jax.experimental.pallas import tpu as pltpu
from jax.sharding import Mesh
from jax.sharding import PartitionSpec as P

HEADS = 16
D = 1024
FF = 4096
ROWS = 256
BLOCK = 128
NA = 8192 + 128
AXES = ("section", "dp_0", "dp_1", "dp_2", "dp_3")
DP = AXES[1:]
MESH = pl.DeviceIdType.MESH
EPSILON = 1e-05
FAR = 1e30
ANY = pl.BlockSpec(memory_space=pl.ANY)
VMEM = pl.BlockSpec(memory_space=pltpu.VMEM)
SMEM = pl.BlockSpec(memory_space=pltpu.SMEM)
bf16 = jnp.bfloat16
f32 = jnp.float32


class Place:
    def __init__(self):
        self.s, self.yh, self.z, self.x, self.c = [lax.axis_index(a) for a in AXES]
        self.p = jnp.where(self.c == 0, self.z, self.x)
        self.q = jnp.where(self.c == 0, self.x, self.z)

    def zx(self, dp, dq):
        pp, qq = lax.rem(self.p + (dp + 4), 4), lax.rem(self.q + (dq + 4), 4)
        return jnp.where(self.c == 0, pp, qq), jnp.where(self.c == 0, qq, pp)

    def at(self, dp, dq):
        z, x = self.zx(dp, dq)
        return (self.s, self.yh, z, x, self.c)

    def half(self, r):
        return lax.rem(self.yh + r, 2)

    def over_y(self):
        return (self.s, 1 - self.yh, self.z, self.x, self.c)

    def other_core(self):
        return (self.s, self.yh, self.z, self.x, 1 - self.c)

    def neighbours(self):
        return (
            self.over_y(),
            self.other_core(),
            self.at(1, 0),
            self.at(-1, 0),
            self.at(0, 1),
            self.at(0, -1),
        )


def greet(devices):
    barrier = pltpu.get_barrier_semaphore()
    for device in devices:
        pl.semaphore_signal(barrier, inc=1, device_id=device, device_id_type=MESH)
    pl.semaphore_wait(barrier, len(devices))


class Mail:
    def __init__(self, send, recv):
        self.send, self.recv, self.sent, self.number = send, recv, [], {}

    def post(self, name, src, dst, device):
        k = self.number.setdefault(name, len(self.number))
        copy = pltpu.make_async_remote_copy(
            src_ref=src,
            dst_ref=dst,
            send_sem=self.send.at[k],
            recv_sem=self.recv.at[k],
            device_id=device,
            device_id_type=MESH,
        )
        copy.start()
        self.sent.append(copy)

    def take(self, name, dst, device):
        k = self.number[name]
        pltpu.make_async_remote_copy(
            src_ref=dst,
            dst_ref=dst,
            send_sem=self.send.at[k],
            recv_sem=self.recv.at[k],
            device_id=device,
            device_id_type=MESH,
        ).wait_recv()

    def finish(self):
        for copy in self.sent:
            copy.wait_send()


GATHER_COPIES = 2 * (1 + 6 + 24 + 32)


def gather_kernel(a_ref, b_ref, ga, gb, send, recv, own):
    at = Place()
    mail = Mail(send, recv)
    greet(at.neighbours())
    outs = (ga, gb)
    local = []
    z0, x0 = at.zx(0, 0)
    for t, (src, out) in enumerate(((a_ref, ga), (b_ref, gb))):
        copy = pltpu.make_async_copy(src, out.at[at.yh, z0, x0, at.c], own.at[t])
        copy.start()
        local.append(copy)

    def view(t, r, dp, dq, core=None):
        z, x = at.zx(dp, dq)
        return outs[t].at[at.half(r), z, x, at.c if core is None else core]

    def post(kind, t, r, dp, dq, device):
        mine = (r, dp, dq) == (0, 0, 0)
        src = (a_ref, b_ref)[t] if mine else view(t, r, dp, dq)
        mail.post((kind, t, r, dp, dq), src, view(t, r, dp, dq), device)

    def spread(r, dq, both=True):
        for t in (0, 1):
            post("PR", t, r, 0, dq, at.at(1, 0))
            post("PL", t, r, 0, dq, at.at(-1, 0))
        hand_over(r, 0, dq)

    def hand_over(r, dp, dq):
        for t in (0, 1):
            post("C", t, r, dp, dq, at.other_core())

    def take(kind, t, sent, got, device):
        mail.take((kind, t, *sent), view(t, *got), device)

    for t in (0, 1):
        post("Y", t, 0, 0, 0, at.over_y())
    for t in (0, 1):
        post("QR", t, 0, 0, 0, at.at(0, 1))
        post("QL", t, 0, 0, 0, at.at(0, -1))
    spread(0, 0)
    for t in (0, 1):
        take("Y", t, (0, 0, 0), (1, 0, 0), at.over_y())
        post("QR", t, 1, 0, 0, at.at(0, 1))
        post("QL", t, 1, 0, 0, at.at(0, -1))
    spread(1, 0)
    for t in (0, 1):
        take("QR", t, (0, 0, 0), (0, 0, -1), at.at(0, 1))
        post("QR2", t, 0, 0, -1, at.at(0, 1))
    spread(0, -1)
    for t in (0, 1):
        take("QL", t, (0, 0, 0), (0, 0, 1), at.at(0, 1))
    spread(0, 1)

    def pass_on(dq):
        for t in (0, 1):
            take("PR", t, (0, 0, dq), (0, -1, dq), at.at(1, 0))
            post("PR2", t, 0, -1, dq, at.at(1, 0))
        for t in (0, 1):
            take("PL", t, (1, 0, dq), (1, 1, dq), at.at(1, 0))
            post("PL2", t, 1, 1, dq, at.at(-1, 0))
        hand_over(0, -1, dq)
        hand_over(1, 1, dq)
        for t in (0, 1):
            take("PL", t, (0, 0, dq), (0, 1, dq), at.at(1, 0))
            take("PR", t, (1, 0, dq), (1, -1, dq), at.at(1, 0))
        hand_over(0, 1, dq)
        hand_over(1, -1, dq)

    for t in (0, 1):
        take("QL", t, (1, 0, 0), (1, 0, 1), at.at(0, 1))
        post("QL2", t, 1, 0, 1, at.at(0, -1))
    spread(1, 1)
    for t in (0, 1):
        take("QR", t, (1, 0, 0), (1, 0, -1), at.at(0, 1))
    spread(1, -1)
    pass_on(0)
    for t in (0, 1):
        take("QR2", t, (0, 0, -1), (0, 0, -2), at.at(0, 1))
    spread(0, 2)
    for t in (0, 1):
        take("QL2", t, (1, 0, 1), (1, 0, 2), at.at(0, 1))
    spread(1, 2)
    for dq in (-1, 1, 2):
        pass_on(dq)
    for dq in (0, -1, 1, 2):
        for t in (0, 1):
            take("PR2", t, (0, -1, dq), (0, -2, dq), at.at(1, 0))
            take("PL2", t, (1, 1, dq), (1, 2, dq), at.at(1, 0))
        hand_over(0, 2, dq)
        hand_over(1, 2, dq)
    for name in [n for n in mail.number if n[0] == "C"]:
        _, t, r, dp, dq = name
        mail.take(name, view(t, r, dq, dp, 1 - at.c), at.other_core())
    mail.finish()
    for copy in local:
        copy.wait()


def gather(a, b):
    return pl.pallas_call(
        gather_kernel,
        out_shape=(
            jax.ShapeDtypeStruct((2, 4, 4, 2, 16, NA), bf16),
            jax.ShapeDtypeStruct((2, 4, 4, 2, 64, D), bf16),
        ),
        in_specs=[ANY, ANY],
        out_specs=(ANY, ANY),
        scratch_shapes=[
            pltpu.SemaphoreType.DMA((GATHER_COPIES,)),
            pltpu.SemaphoreType.DMA((GATHER_COPIES,)),
            pltpu.SemaphoreType.DMA((2,)),
        ],
        compiler_params=pltpu.CompilerParams(collective_id=0, has_side_effects=True),
        name="gather_weights",
    )(a, b)


def dot(a, b, dims=((1,), (0,))):
    return lax.dot_general(a, b, (dims, ((), ())), preferred_element_type=f32)


NT = ((1,), (1,))
TN = ((0,), (0,))


def cols(j, width):
    return pl.ds(pl.multiple_of(j * width, width), width)


B_QUERY, B_VALUE, B_OUT, B_DOWN, G_ONE, S_ONE, G_TWO, S_TWO = range(8)


def layer_kernel(
    tokens,
    places,
    cotangent,
    slopes,
    vec,
    b_up,
    w_rows,
    w_down,
    layer_out,
    input_grad,
    n_t,
    a_t,
    n2_t,
    act_t,
    g_mixed,
    g_branch,
    g_upward,
    g_y,
    g_vec,
    g_bup,
    xin,
    gyin,
    gxout,
    w1,
    w2,
    xhat1,
    rstd1,
    xhat2,
    rstd2,
    mixed,
    far,
    probs,
    wide,
    middle,
    gprime,
    act,
    grad,
    load,
    send,
    recv,
):
    section = lax.axis_index("section")
    loads = {}
    pieces = [("qkv", j * 1024, 1024) for j in range(3)]
    pieces += [("out", 3072, 1024)] + [("up", 4096 + j * 1024, 1024) for j in range(4)]
    for k, (name, at, width) in enumerate(pieces):
        copy = pltpu.make_async_copy(
            w_rows.at[:, pl.ds(at, width)], w1.at[:, pl.ds(at, width)], load.at[k]
        )
        copy.start()
        loads.setdefault(name, []).append(copy)
    copy = pltpu.make_async_copy(w_down, w2, load.at[len(pieces)])
    copy.start()
    loads["down"] = [copy]

    def loaded(name):
        for item in loads[name]:
            item.wait()

    other = {"section": 1 - section}
    greet((other,))
    forth = pltpu.make_async_remote_copy(
        src_ref=layer_out,
        dst_ref=xin,
        send_sem=send.at[0],
        recv_sem=recv.at[0],
        device_id=other,
        device_id_type=MESH,
    )
    back = pltpu.make_async_remote_copy(
        src_ref=gxout,
        dst_ref=gyin,
        send_sem=send.at[1],
        recv_sem=recv.at[1],
        device_id=other,
        device_id_type=MESH,
    )

    row = lax.broadcasted_iota(jnp.int32, (BLOCK, BLOCK), 0)
    col = lax.broadcasted_iota(jnp.int32, (BLOCK, BLOCK), 1)
    distance = row - col
    for b in range(2):
        allowed = (distance >= 0) & (distance <= places[pl.ds(b * BLOCK, BLOCK), :])
        far[b] = jnp.where(allowed, distance.astype(f32), FAR)
    low_lane = lax.broadcasted_iota(jnp.int32, (BLOCK, BLOCK), 1) < 64

    @pl.when(section == 0)
    def _():
        xin[...] = tokens[...]

    @pl.when(section == 1)
    def _():
        forth.wait_recv()
        gyin[...] = cotangent[...]

    chunk = 32

    def rows_loop(body):
        @pl.loop(0, ROWS // chunk)
        def _(i):
            body(pl.ds(pl.multiple_of(i * chunk, chunk), chunk))

    def norm_rows(rows, v, xhat, rstd, gain, shift):
        center = v - jnp.mean(v, axis=-1, keepdims=True)
        r = lax.rsqrt(jnp.mean(center * center, axis=-1, keepdims=True) + EPSILON)
        h = center * r
        xhat[rows, :] = h
        rstd[rows, :] = jnp.broadcast_to(r, (chunk, 128))
        return h * vec[pl.ds(gain, 1), :] + vec[pl.ds(shift, 1), :]

    def transpose_into(dst, src, width):
        @pl.loop(0, width // 256)
        def _(j):
            dst[cols(j, 256), :] = src[:, cols(j, 256)].T

    def one(rows):
        v = xin[rows, :].astype(f32)
        g_branch[rows, :] = norm_rows(rows, v, xhat1, rstd1, G_ONE, S_ONE).astype(bf16)

    rows_loop(one)
    transpose_into(n_t, g_branch, D)

    loaded("qkv")

    @pl.loop(0, 6)
    def _(j):
        y = dot(g_branch[...], w1[:, cols(j, 512)])
        mixed[:, cols(j, 512)] = (y + wide[pl.ds(0, 1), cols(j, 512)]).astype(bf16)

    def pair(value):
        zero = jnp.zeros_like(value)
        return jnp.concatenate(
            [jnp.where(low_lane, value, zero), jnp.where(low_lane, zero, value)], axis=0
        )

    def unpair(value):
        return jnp.where(low_lane, value[:BLOCK], value[BLOCK:])

    def slope_rows(hp):
        first = lax.broadcasted_iota(jnp.int32, (2 * BLOCK, 1), 0) < BLOCK
        return jnp.where(first, slopes[2 * hp], slopes[2 * hp + 1])

    def heads(ref, b, part, hp):
        at = pl.multiple_of(part * D + hp * 128, 128)
        return ref[pl.ds(b * BLOCK, BLOCK), pl.ds(at, 128)]

    @pl.loop(0, 8)
    def _(hp):
        for b in range(2):
            queries = pair(heads(mixed, b, 0, hp))
            scores = dot(queries, heads(mixed, b, 1, hp), NT) * 0.125
            gap = jnp.concatenate([far[b], far[b]], axis=0)
            scores = scores - slope_rows(hp) * gap
            e = jnp.exp(scores - jnp.max(scores, axis=-1, keepdims=True))
            p = e * (1.0 / jnp.sum(e, axis=-1, keepdims=True))
            probs[2 * hp + b] = p
            out = unpair(dot(p.astype(bf16), heads(mixed, b, 2, hp)))
            g_y[pl.ds(b * BLOCK, BLOCK), pl.ds(pl.multiple_of(hp * 128, 128), 128)] = (
                out.astype(bf16)
            )

    transpose_into(a_t, g_y, D)
    loaded("out")

    @pl.loop(0, 2)
    def _(j):
        y = dot(g_y[...], w1[:, pl.ds(pl.multiple_of(3072 + j * 512, 512), 512)])
        middle[:, cols(j, 512)] = (
            xin[:, cols(j, 512)].astype(f32) + y + vec[pl.ds(B_OUT, 1), cols(j, 512)]
        )

    def two(rows):
        g_branch[rows, :] = norm_rows(
            rows, middle[rows, :], xhat2, rstd2, G_TWO, S_TWO
        ).astype(bf16)

    rows_loop(two)
    transpose_into(n2_t, g_branch, D)
    loaded("up")

    @pl.loop(0, 8)
    def _(j):
        y = dot(g_branch[...], w1[:, pl.ds(pl.multiple_of(4096 + j * 512, 512), 512)])
        u = y + b_up[pl.ds(0, 1), cols(j, 512)]
        c = 0.7978845608028654
        uu = u * u
        t = jnp.tanh(c * (u + 0.044715 * u * uu))
        half = 0.5 * (1.0 + t)
        a = (u * half).astype(bf16)
        act[:, cols(j, 512)] = a
        act_t[cols(j, 512), :] = a.T
        gprime[:, cols(j, 512)] = half + 0.5 * u * (1.0 - t * t) * (
            c * (1.0 + (3 * 0.044715) * uu)
        )

    loaded("down")

    @pl.loop(0, 2)
    def _(j):
        y = dot(act[...], w2[:, cols(j, 512)])
        y = middle[:, cols(j, 512)] + y + vec[pl.ds(B_DOWN, 1), cols(j, 512)]
        layer_out[:, cols(j, 512)] = y.astype(bf16)

    @pl.when(section == 0)
    def _():
        forth.start()
        back.wait_recv()

    g_y[...] = gyin[...]
    g_vec[...] = jnp.zeros_like(g_vec)

    @pl.loop(0, 8)
    def _(j):
        g = dot(g_y[...], w2[cols(j, 512), :], NT)
        g = (g * gprime[:, cols(j, 512)]).astype(bf16)
        g_upward[:, cols(j, 512)] = g
        g_bup[:, cols(j, 512)] = jnp.broadcast_to(
            jnp.sum(g.astype(f32), axis=0, keepdims=True), (8, 512)
        )

    @pl.loop(0, 4)
    def _(j):
        grad[:, cols(j, 256)] = dot(g_upward[...], w1[cols(j, 256), pl.ds(4096, 4096)], NT)

    def add(index, value):
        g_vec[pl.ds(index, 1), :] = g_vec[pl.ds(index, 1), :] + jnp.sum(
            value, axis=0, keepdims=True
        )

    def norm_back(rows, xhat, rstd, gain, shift):
        dy = grad[rows, :]
        h = xhat[rows, :]
        add(gain, dy * h)
        add(shift, dy)
        dh = dy * vec[pl.ds(gain, 1), :]
        m1 = jnp.mean(dh, axis=-1, keepdims=True)
        m2 = jnp.mean(dh * h, axis=-1, keepdims=True)
        return rstd[rows, pl.ds(0, 1)] * (dh - m1 - h * m2)

    def three(rows):
        gy = g_y[rows, :].astype(f32)
        gm = gy + norm_back(rows, xhat2, rstd2, G_TWO, S_TWO)
        add(B_DOWN, gy)
        middle[rows, :] = gm
        low = gm.astype(bf16)
        g_branch[rows, :] = low
        add(B_OUT, low.astype(f32))

    rows_loop(three)

    @pl.loop(0, 4)
    def _(j):
        y = dot(g_branch[...], w1[cols(j, 256), pl.ds(3072, 1024)], NT)
        act[:, cols(j, 256)] = y.astype(bf16)

    @pl.loop(0, 8)
    def _(hp):
        for b in range(2):
            queries = pair(heads(mixed, b, 0, hp))
            keys, values = heads(mixed, b, 1, hp), heads(mixed, b, 2, hp)
            da = pair(heads(act, b, 0, hp))
            p = probs[2 * hp + b]
            dv = dot(p.astype(bf16), da, TN)
            dp = dot(da, values, NT)
            delta = jnp.sum(p * dp, axis=-1, keepdims=True)
            ds = (p * (dp - delta)).astype(bf16)
            dq = unpair(dot(ds, keys)) * 0.125
            dk = dot(ds, queries, TN) * 0.125
            for part, value in enumerate((dq, dk, dv)):
                at = pl.multiple_of(part * D + hp * 128, 128)
                g_mixed[pl.ds(b * BLOCK, BLOCK), pl.ds(at, 128)] = value.astype(bf16)

    @pl.loop(0, 4)
    def _(j):
        grad[:, cols(j, 256)] = dot(g_mixed[...], w1[cols(j, 256), pl.ds(0, 3072)], NT)

    def four(rows):
        gx = middle[rows, :] + norm_back(rows, xhat1, rstd1, G_ONE, S_ONE)
        gxout[rows, :] = gx.astype(bf16)
        add(B_QUERY, g_mixed[rows, pl.ds(0, D)].astype(f32))
        add(B_VALUE, g_mixed[rows, pl.ds(2 * D, D)].astype(f32))

    rows_loop(four)

    @pl.when(section == 1)
    def _():
        back.start()

    input_grad[...] = gxout[...]

    @pl.when(section == 0)
    def _():
        forth.wait_send()

    @pl.when(section == 1)
    def _():
        back.wait_send()


def layer_kernel_with_bias(tokens, places, cotangent, slopes, vec, *refs):
    wide = refs[SCRATCH_WIDE]
    wide[pl.ds(0, 1), pl.ds(0, D)] = vec[pl.ds(B_QUERY, 1), :]
    wide[pl.ds(0, 1), pl.ds(D, D)] = jnp.zeros((1, D), f32)
    wide[pl.ds(0, 1), pl.ds(2 * D, D)] = vec[pl.ds(B_VALUE, 1), :]
    layer_kernel(tokens, places, cotangent, slopes, vec, *refs)


SCRATCH_WIDE = 3 + 12 + 12


def layer(tokens, places, cotangent, slopes, vec, b_up, w_rows, w_down):
    def out(rows, columns, kind=bf16):
        return jax.ShapeDtypeStruct((rows, columns), kind)

    return pl.pallas_call(
        layer_kernel_with_bias,
        out_shape=(
            out(ROWS, D),
            out(ROWS, D),
            out(D, ROWS),
            out(D, ROWS),
            out(D, ROWS),
            out(FF, ROWS),
            out(ROWS, 3 * D),
            out(ROWS, D),
            out(ROWS, FF),
            out(ROWS, D),
            out(8, D, f32),
            out(8, FF, f32),
        ),
        in_specs=[VMEM, VMEM, VMEM, SMEM, VMEM, VMEM, ANY, ANY],
        out_specs=(VMEM,) * 12,
        scratch_shapes=[
            pltpu.VMEM((ROWS, D), bf16),
            pltpu.VMEM((ROWS, D), bf16),
            pltpu.VMEM((ROWS, D), bf16),
            pltpu.VMEM((D, 8192), bf16),
            pltpu.VMEM((FF, D), bf16),
            pltpu.VMEM((ROWS, D), f32),
            pltpu.VMEM((ROWS, 128), f32),
            pltpu.VMEM((ROWS, D), f32),
            pltpu.VMEM((ROWS, 128), f32),
            pltpu.VMEM((ROWS, 3 * D), bf16),
            pltpu.VMEM((2, BLOCK, BLOCK), f32),
            pltpu.VMEM((16, 2 * BLOCK, BLOCK), f32),
            pltpu.VMEM((8, 3 * D), f32),
            pltpu.VMEM((ROWS, D), f32),
            pltpu.VMEM((ROWS, FF), f32),
            pltpu.VMEM((ROWS, FF), bf16),
            pltpu.VMEM((ROWS, D), f32),
            pltpu.SemaphoreType.DMA((9,)),
            pltpu.SemaphoreType.DMA((2,)),
            pltpu.SemaphoreType.DMA((2,)),
        ],
        compiler_params=pltpu.CompilerParams(
            collective_id=1, has_side_effects=True, vmem_limit_bytes=60 * 2**20
        ),
        name="layer",
    )(tokens, places, cotangent, slopes, vec, b_up, w_rows, w_down)


KINDS = ((64, D), (16, FF), (16, 3 * D), (16, D))
SCATTER_COPIES = 4 * (2 + 6 + 6 + 1)


def scatter_kernel(*refs):
    lhs_in, rhs_in, outs = refs[0:4], refs[4:8], refs[8:12]
    lhs, rhs, own, ring_p, ring_q, last = [refs[12 + 4 * k : 16 + 4 * k] for k in range(6)]
    block, block_down, send, recv, load = refs[36:]
    at = Place()
    mail = Mail(send, recv)
    greet(at.neighbours())
    local = []
    for a in range(4):
        here, there = pl.ds(0, ROWS), pl.ds(ROWS, ROWS)
        mail.post(
            ("L", a),
            lhs_in[a].at[:, :, :, 1 - at.c],
            lhs[a].at[:, :, :, :, there],
            at.other_core(),
        )
        mail.post(("R", a), rhs_in[a], rhs[a].at[there, :], at.other_core())
        copies = (
            pltpu.make_async_copy(
                lhs_in[a].at[:, :, :, at.c], lhs[a].at[:, :, :, :, here], load.at[2 * a]
            ),
            pltpu.make_async_copy(rhs_in[a], rhs[a].at[here, :], load.at[2 * a + 1]),
        )
        for copy in copies:
            copy.start()
        local.append(copies)

    def ready(a):
        there = pl.ds(ROWS, ROWS)
        mail.take(("L", a), lhs[a].at[:, :, :, :, there], at.other_core())
        mail.take(("R", a), rhs[a].at[there, :], at.other_core())
        for copy in local[a]:
            copy.wait()

    def products(a, d):
        rows, width = KINDS[a]
        buffer = block_down if rows == 64 else block
        for r in range(2):
            for e in range(4):
                z, x = at.zx(d, e)
                buffer[pl.ds((r * 4 + e) * rows, rows), :] = lhs[a][at.half(r), z, x]

        @pl.loop(0, width // 512)
        def _(j):
            y = dot(buffer[...], rhs[a][:, cols(j, 512)])
            own[a][:, d, :, :, cols(j, 512)] = y.reshape(2, 4, rows, 512).astype(bf16)

    def total(a, dst, terms):
        @pl.loop(0, KINDS[a][1] // 512)
        def _(j):
            value = None
            for term in terms:
                piece = term[..., cols(j, 512)].astype(f32)
                value = piece if value is None else value + piece
            dst[..., cols(j, 512)] = value.astype(dst.dtype)

    right_p, left_p = at.at(1, 0), at.at(-1, 0)
    right_q, left_q = at.at(0, 1), at.at(0, -1)

    def post_p(a, k, r, d, device):
        mail.post(("P", a, k), own[a].at[r, d], ring_p[a].at[k], device)

    def take_p(a, k):
        mail.take(("P", a, k), ring_p[a].at[k], right_p)

    def post_q(a, k, r, e, device):
        mail.post(("Q", a, k), own[a].at[r, 0, e], ring_q[a].at[k], device)

    def take_q(a, k):
        mail.take(("Q", a, k), ring_q[a].at[k], right_q)

    def sum_into(a, dst, *terms):
        total(a, dst, (dst, *terms))

    for a in range(4):
        ready(a)
        products(a, 2)
        post_p(a, 0, 0, 2, right_p)
        post_p(a, 1, 1, 2, left_p)
        products(a, 1)
        post_p(a, 2, 1, 1, right_p)
        products(a, 3)
        post_p(a, 3, 0, 3, left_p)
    for a in range(4):
        take_p(a, 0)
        sum_into(a, own[a].at[0, 1], ring_p[a].at[0])
        post_p(a, 4, 0, 1, right_p)
        take_p(a, 1)
        sum_into(a, own[a].at[1, 3], ring_p[a].at[1])
        post_p(a, 5, 1, 3, left_p)
        products(a, 0)
    for a in range(4):
        for k in (2, 3, 4, 5):
            take_p(a, k)
        sum_into(a, own[a].at[0, 0], ring_p[a].at[4], ring_p[a].at[3])
        sum_into(a, own[a].at[1, 0], ring_p[a].at[2], ring_p[a].at[5])
        post_q(a, 0, 0, 2, right_q)
        post_q(a, 1, 1, 2, left_q)
        post_q(a, 2, 1, 1, right_q)
        post_q(a, 3, 0, 3, left_q)
    for a in range(4):
        take_q(a, 0)
        sum_into(a, own[a].at[0, 0, 1], ring_q[a].at[0])
        post_q(a, 4, 0, 1, right_q)
        take_q(a, 1)
        sum_into(a, own[a].at[1, 0, 3], ring_q[a].at[1])
        post_q(a, 5, 1, 3, left_q)
    for a in range(4):
        for k in (2, 3, 4, 5):
            take_q(a, k)
        sum_into(a, own[a].at[1, 0, 0], ring_q[a].at[2], ring_q[a].at[5])
        mail.post(("Y", a), own[a].at[1, 0, 0], last[a], at.over_y())
    for a in range(4):
        mail.take(("Y", a), last[a], at.over_y())
        terms = (own[a].at[0, 0, 0], ring_q[a].at[4], ring_q[a].at[3], last[a])
        total(a, outs[a], terms)
    mail.finish()


def scatter(lhs, rhs):
    def scratch(*lead):
        return [pltpu.VMEM((*lead, rows, width), bf16) for rows, width in KINDS]

    return pl.pallas_call(
        scatter_kernel,
        out_shape=tuple(jax.ShapeDtypeStruct(kind, f32) for kind in KINDS),
        in_specs=[ANY] * 8,
        out_specs=(VMEM,) * 4,
        scratch_shapes=[
            *[pltpu.VMEM((2, 4, 4, rows, 2 * ROWS), bf16) for rows, _ in KINDS],
            *[pltpu.VMEM((2 * ROWS, width), bf16) for _, width in KINDS],
            *scratch(2, 4, 4),
            *scratch(6, 4),
            *scratch(6),
            *scratch(),
            pltpu.VMEM((128, 2 * ROWS), bf16),
            pltpu.VMEM((512, 2 * ROWS), bf16),
            pltpu.SemaphoreType.DMA((SCATTER_COPIES,)),
            pltpu.SemaphoreType.DMA((SCATTER_COPIES,)),
            pltpu.SemaphoreType.DMA((8,)),
        ],
        compiler_params=pltpu.CompilerParams(
            collective_id=2, has_side_effects=True, vmem_limit_bytes=60 * 2**20
        ),
        name="scatter_gradients",
    )(*lhs, *rhs)


def body(
    tokens,
    positions,
    cotangent,
    w_qkv,
    b_query,
    b_value,
    w_out,
    b_out,
    w_up,
    b_up,
    w_down,
    b_down,
    gain_one,
    shift_one,
    gain_two,
    shift_two,
):
    small = (b_query, b_value, b_out, b_down, gain_one, shift_one, gain_two, shift_two)
    packed = jnp.concatenate([b_up, *small], axis=1)
    packed = jnp.pad(packed, ((0, 0), (0, 2048 - 192))).reshape(16, 128)
    ga, gb = gather(jnp.concatenate([w_qkv[0], w_out[0], w_up[0], packed], axis=1), w_down[0])
    ga, gb = ga.reshape(D, NA), gb.reshape(FF, D)
    vectors = ga[:, 8192:].reshape(64, 2048)[:, :192].astype(f32)
    bup_all = vectors[:, :64].reshape(1, FF)
    vec_all = vectors[:, 64:].reshape(64, 8, 16).transpose(1, 0, 2).reshape(8, D)
    slopes = 2.0 ** (-8.0 * jnp.arange(1, HEADS + 1, dtype=f32) / HEADS)
    results = layer(
        tokens.reshape(ROWS, D),
        positions.reshape(ROWS, 1),
        cotangent.reshape(ROWS, D),
        slopes,
        vec_all,
        jnp.broadcast_to(bup_all, (8, FF)),
        ga,
        gb,
    )
    layer_out, input_grad, n_t, a_t, n2_t, act_t, g_mixed, g_branch, g_up, g_y, g_vec, g_bup = results

    def shards(value, rows):
        return value.reshape(2, 4, 4, 2, rows, ROWS)

    down, up, qkv, out = scatter(
        (shards(act_t, 64), shards(n2_t, 16), shards(n_t, 16), shards(a_t, 16)),
        (g_y, g_up, g_mixed, g_branch),
    )
    own_vec = g_vec.reshape(8, 64, 16).transpose(1, 0, 2).reshape(64, 128)
    both = jnp.concatenate([g_bup[0].reshape(64, 64), own_vec], axis=1)
    mine = lax.psum_scatter(both, DP, scatter_dimension=0, tiled=True)
    gbu, rest = mine[:, :64], mine[:, 64:]
    gv = [rest[:, 16 * k : 16 * k + 16] for k in range(8)]
    return (
        layer_out.reshape(1, 2, BLOCK, D),
        input_grad.reshape(1, 2, BLOCK, D),
        qkv[None],
        gv[B_QUERY],
        gv[B_VALUE],
        out[None],
        gv[B_OUT],
        up[None],
        gbu,
        down[None],
        gv[B_DOWN],
        gv[G_ONE],
        gv[S_ONE],
        gv[G_TWO],
        gv[S_TWO],
    )


def solution(mesh):
    torus = Mesh(mesh.devices.reshape(2, 2, 4, 4, 2), AXES)
    rows, matrix, vector = P(None, DP, None), P("section", DP, None), P("section", DP)
    of_layer = P("section", None, DP, None)
    return jax.shard_map(
        body,
        mesh=torus,
        in_specs=(
            rows,
            P(None, DP),
            rows,
            matrix,
            vector,
            vector,
            matrix,
            vector,
            matrix,
            vector,
            matrix,
            vector,
            vector,
            vector,
            vector,
            vector,
        ),
        out_specs=(
            of_layer,
            of_layer,
            matrix,
            vector,
            vector,
            matrix,
            vector,
            matrix,
            vector,
            matrix,
            vector,
            vector,
            vector,
            vector,
            vector,
        ),
        check_vma=False,
    )
```

time: 1550 us -> 627 us (0.40)
  waiting for transfers between devices: 874 us -> 0 us
  Pallas kernels: 0 us -> 276 us
  matrix products: 256 us -> 0 us
  local copies, waits for them, and re-layouts: 82.4 us -> 17.8 us
  blocking collectives: 284 us -> 330 us
  between operations: 16.8 us -> 0.82 us
  other arithmetic: 18.2 us -> 2.24 us
    reduce_scatter x9 -> x0, waiting for transfers between devices: 662 us -> none  [the longest x4 635 us: scatter_pairs(): return lax.psum_scatter(pieces, chips, scatter_dimension=0, tiled=True)[0]]
    pallas_call x0 -> x3, Pallas kernels: none -> 276 us  [the longest x1 117 us: layer(): pl.pallas_call(layer_kernel_with_bias, out_shape=(out(ROWS, D), out(ROWS,...]
    dot_general x54 -> x0, matrix products: 256 us -> none  [the longest x3 44 us: backward_layer(): jnp.dot(activated.T, upstream, preferred_element_type=jnp.float32)]
    unnamed x1, blocking collectives: 186 us -> 330 us
    unnamed x27 -> x0, waiting for transfers between devices: 101 us -> none
    all_gather x1 -> x0, blocking collectives: 98.2 us -> none  [in_one_piece(): lax.all_gather(both, axis, axis=dim, tiled=True)]
    all_gather x2 -> x0, waiting for transfers between devices: 90.4 us -> none  [side_by_side(): out = lax.all_gather(both, axis, axis=dim, tiled=True)]
    transpose x5 -> x2, local copies, waits for them, and re-layouts: 37 us -> 0.24 us  [the longest x1 0.13 us: body(): vectors[:, 64:].reshape(64, 8, 16).transpose(1, 0, 2).reshape(8, D)]
  transfers between devices with their start and end apart: 23 -> 0, of which waited for: 18 -> 0; matrix products, arithmetic and copies ran while one was open for 13% -> 0% of each run, Pallas kernels for 0% -> 0%
where the time goes in v1:
time: 627 us
  blocking collectives  330 us (53%)
  Pallas kernels  276 us (44%)
  local copies, waits for them, and re-layouts  17.8 us (3%)
    unnamed x1, blocking collectives  330 us
    pallas_call x1, Pallas kernels, layer(): pl.pallas_call(layer_kernel_with_bias, out_shape=(out(ROWS, D), out(ROWS,...  117 us
    pallas_call x1, Pallas kernels, scatter(): pl.pallas_call(scatter_kernel, out_shape=tuple((jax.ShapeDtypeStruct(kind...  79.5 us
    pallas_call x1, Pallas kernels, gather(): pl.pallas_call(gather_kernel, out_shape=(jax.ShapeDtypeStruct((2, 4, 4, 2...  79.2 us

profile of v1, /device:TPU:0, one launch (start us, length us, event | category | flops | bytes accessed | tf_op | source)
XLA Modules:
  0.0 627.2 jit_solution(14412574422409464344)
XLA Ops:
  0.6 0.0 copy-start.7
  0.7 0.9 concatenate.9
  1.6 1.7 pad_maximum_fusion.a_ref
  3.3 79.2 %gather_weights.1 = (bf16[2,4,4,2,16,8320]{5,4,3,2,1,0:T(8,128)(2,1)}, bf16[2,4,4,2,64,1024]{5,4,3,2,1,0:T(8,128)(2,1)}) custom-call(bf16[16,8320]{1,0:T(8,128)(2,1)} %pad_maximum_fusion.a_ref, bf16[64,1024]{1,0:T(8,128)(2,1)} %bitcast.45), custom_call_target="tpu_custom_call" | custom-call | tf_op jit(solution)/shard_map/gather_weights/pallas_call | solution.py:205
  82.5 1.0 slice.65
  83.5 0.1 reshape.88
  83.6 0.1 slice.67
  83.7 0.1 copy.80
  83.8 0.1 copy.63
  83.9 0.8 reshape.90.vec
  84.7 0.1 copy.81
  84.8 0.1 copy.64
  84.8 0.1 broadcast_in_dim.19
  84.9 0.7 broadcast_in_dim.20.refs_0_
  85.6 0.8 copy.65.places
  86.4 0.5 multiply_power_fusion.slopes
  86.9 117.2 %layer.1 = (bf16[256,1024]{1,0:T(8,128)(2,1)}, bf16[256,1024]{1,0:T(8,128)(2,1)}, bf16[1024,256]{1,0:T(8,128)(2,1)}, bf16[1024,256]{1,0:T(8,128)(2,1)}, bf16[102...) custom-call(bf16[256,1024]{1,0:T(8,128)(2,1)} %bitcast.33, ...), custom_call_target="tpu_custom_call" | custom-call | tf_op jit(solution)/shard_map/layer/pallas_call | solution.py:553
  204.2 0.0 copy-start.8
  204.2 0.0 copy-start.1
  204.2 79.5 %scatter_gradients.1 = (f32[64,1024]{1,0:T(8,128)}, f32[16,4096]{1,0:T(8,128)}, f32[16,3072]{1,0:T(8,128)}, f32[16,1024]{1,0:T(8,128)}) custom-call(bf16[2,4,4,2,64,256]{5,4,3,2,1,0:T(8,128)(2,1)} %bitcast.31, bf16[2,4,4,2,16,256]{5,4,3,2,1,0:T(8,128)(2,1)} %bitcast.37, bf16[2,4,4,2,16,256]{5,4,3,2,1,0:T(8,128)(2,1)} %bitcast.35, ...), custom_call_target="tpu_custom_call" | custom-call | tf_op jit(solution)/shard_map/scatter_gradients/pallas_call | solution.py:727
  283.6 0.0 copy-start
  283.7 0.0 copy-start.4
  283.7 0.0 copy-start.5
  283.7 0.0 copy-start.3
  283.7 0.1 reshape.98
  283.8 0.1 copy.66
  283.9 1.0 slice_reduce_fusion
  284.9 0.1 reshape_squeeze.3
  285.0 0.1 copy.67
  285.1 330.5 %all-reduce.1 = f32[64,192]{0,1:T(8,128)S(1)} all-reduce(f32[64,192]{0,1:T(8,128)S(1)} %pad_maximum_fusion.1), channel_id=2, replica_groups=mesh['section'=2,'dp_0'=2,'dp_1'=4,'dp_2'=4,'dp_3'=2] {'dp_0','dp_1','dp..., use_global_device_ids=true, to_apply=%region_0.1.clone | all-reduce | flops 12288 | bytes 98304
  615.6 0.6 dynamic-slice
  616.2 0.7 fusion
  616.9 0.6 copy.68
  617.5 0.6 copy.69
  618.1 0.6 copy.70
  618.7 0.6 copy.72
  619.2 0.6 copy.73
  619.8 0.6 copy.74
  620.4 0.6 copy.75
  621.0 0.6 copy.76
  621.6 0.7 constant_dynamic-slice_fusion
  622.3 0.6 copy.71
  622.9 0.8 copy.88
  623.7 0.8 copy.89
  624.5 0.7 copy.90
  625.2 0.6 copy.91
  625.8 0.7 copy.92
  626.5 0.7 copy.93
  (15 shorter events, 0.1 us)
Async XLA Ops:
  0.6 84.9 %copy-start.7 = (s32[2,128]{1,0:T(2,128)S(1)}, s32[2,128]{1,0:T(2,128)}, u32[]{:S(2)}) copy-start(s32[2,128]{1,0:T(2,128)} %param.17) | copy-start | bytes 3076
  204.1 79.5 %copy-start.6 = (f32[8,1024]{1,0:T(8,128)S(1)}, f32[8,1024]{1,0:T(8,128)}, u32[]{:S(2)}) copy-start(f32[8,1024]{1,0:T(8,128)} %get-tuple-element.47) | copy-start | bytes 98308
  204.2 411.4 %copy-start.8 = (u32[128]{0:T(128)S(1)}, u32[128]{0:T(128)}, u32[]{:S(2)}) copy-start(u32[128]{0:T(128)} %constant.29) | copy-start | bytes 1540
  204.2 418.7 %copy-start.1 = (bf16[256,1024]{1,0:T(8,128)(2,1)S(1)}, bf16[256,1024]{1,0:T(8,128)(2,1)}, u32[]{:S(2)}) copy-start(bf16[256,1024]{1,0:T(8,128)(2,1)} %get-tuple-element.35) | copy-start | bytes 1572868
  283.6 340.0 %copy-start = (bf16[256,1024]{1,0:T(8,128)(2,1)S(1)}, bf16[256,1024]{1,0:T(8,128)(2,1)}, u32[]{:S(2)}) copy-start(bf16[256,1024]{1,0:T(8,128)(2,1)} %get-tuple-element.36) | copy-start | bytes 1572868
  283.7 340.8 %copy-start.4 = (f32[16,3072]{1,0:T(8,128)S(1)}, f32[16,3072]{1,0:T(8,128)}, u32[]{:S(2)}) copy-start(f32[16,3072]{1,0:T(8,128)} %get-tuple-element.45) | copy-start | bytes 589828
  283.7 341.5 %copy-start.5 = (f32[16,1024]{1,0:T(8,128)S(1)}, f32[16,1024]{1,0:T(8,128)}, u32[]{:S(2)}) copy-start(f32[16,1024]{1,0:T(8,128)} %get-tuple-element.48) | copy-start | bytes 196612
  283.7 342.1 %copy-start.3 = (f32[16,4096]{1,0:T(8,128)S(1)}, f32[16,4096]{1,0:T(8,128)}, u32[]{:S(2)}) copy-start(f32[16,4096]{1,0:T(8,128)} %get-tuple-element.49) | copy-start | bytes 786436
  283.9 342.6 %copy-start.2 = (f32[64,1024]{1,0:T(8,128)S(1)}, f32[64,1024]{1,0:T(8,128)}, u32[]{:S(2)}) copy-start(f32[64,1024]{1,0:T(8,128)} %get-tuple-element.50) | copy-start | bytes 786436

commit v2 on v1

--- a/solution.py
+++ b/solution.py
@@ -255,7 +255,6 @@
     g_upward,
     g_y,
     g_vec,
-    g_bup,
     xin,
     gyin,
     gxout,
@@ -452,8 +451,8 @@
         g = dot(g_y[...], w2[cols(j, 512), :], NT)
         g = (g * gprime[:, cols(j, 512)]).astype(bf16)
         g_upward[:, cols(j, 512)] = g
-        g_bup[:, cols(j, 512)] = jnp.broadcast_to(
-            jnp.sum(g.astype(f32), axis=0, keepdims=True), (8, 512)
+        g_vec[pl.ds(8 + j // 2, 1), cols(j % 2, 512)] = jnp.sum(
+            g.astype(f32), axis=0, keepdims=True
         )
 
     @pl.loop(0, 4)
@@ -543,7 +542,7 @@
     layer_kernel(tokens, places, cotangent, slopes, vec, *refs)
 
 
-SCRATCH_WIDE = 3 + 12 + 12
+SCRATCH_WIDE = 3 + 11 + 12
 
 
 def layer(tokens, places, cotangent, slopes, vec, b_up, w_rows, w_down):
@@ -563,11 +562,10 @@
             out(ROWS, D),
             out(ROWS, FF),
             out(ROWS, D),
-            out(8, D, f32),
-            out(8, FF, f32),
+            out(16, D, f32),
         ),
         in_specs=[VMEM, VMEM, VMEM, SMEM, VMEM, VMEM, ANY, ANY],
-        out_specs=(VMEM,) * 12,
+        out_specs=(VMEM,) * 11,
         scratch_shapes=[
             pltpu.VMEM((ROWS, D), bf16),
             pltpu.VMEM((ROWS, D), bf16),
@@ -598,16 +596,35 @@
 
 
 KINDS = ((64, D), (16, FF), (16, 3 * D), (16, D))
-SCATTER_COPIES = 4 * (2 + 6 + 6 + 1)
+SCATTER_COPIES = 4 * (2 + 6 + 6 + 1) + 6
 
 
 def scatter_kernel(*refs):
-    lhs_in, rhs_in, outs = refs[0:4], refs[4:8], refs[8:12]
-    lhs, rhs, own, ring_p, ring_q, last = [refs[12 + 4 * k : 16 + 4 * k] for k in range(6)]
-    block, block_down, send, recv, load = refs[36:]
+    lhs_in, rhs_in, vec_in, outs, vec_out = refs[0:4], refs[4:8], refs[8], refs[9:13], refs[13]
+    lhs, rhs, own, ring_p, ring_q, last = [refs[14 + 4 * k : 18 + 4 * k] for k in range(6)]
+    block, block_down, vec_sum, vec_got, send, recv, load = refs[38:]
     at = Place()
     mail = Mail(send, recv)
     greet(at.neighbours())
+    even_p, even_q = 1 - 2 * lax.rem(at.p, 2), 1 - 2 * lax.rem(at.q, 2)
+    partners = (
+        at.other_core(),
+        at.at(even_p, 0),
+        at.at(-even_p, 0),
+        at.at(0, even_q),
+        at.at(0, -even_q),
+        at.over_y(),
+    )
+
+    def post_vec(k):
+        mail.post(("V", k), vec_sum.at[k], vec_got.at[k], partners[k])
+
+    def take_vec(k):
+        mail.take(("V", k), vec_got.at[k], partners[k])
+        vec_sum[k + 1] = vec_sum[k] + vec_got[k]
+
+    vec_sum[0] = vec_in[...]
+    post_vec(0)
     local = []
     for a in range(4):
         here, there = pl.ds(0, ROWS), pl.ds(ROWS, ROWS)
@@ -632,6 +649,9 @@
         there = pl.ds(ROWS, ROWS)
         mail.take(("L", a), lhs[a].at[:, :, :, :, there], at.other_core())
         mail.take(("R", a), rhs[a].at[there, :], at.other_core())
+        if a == 0:
+            take_vec(0)
+            post_vec(1)
         for copy in local[a]:
             copy.wait()
 
@@ -691,6 +711,8 @@
         take_p(a, 1)
         sum_into(a, own[a].at[1, 3], ring_p[a].at[1])
         post_p(a, 5, 1, 3, left_p)
+        take_vec(a + 1)
+        post_vec(a + 2)
         products(a, 0)
     for a in range(4):
         for k in (2, 3, 4, 5):
@@ -713,6 +735,8 @@
             take_q(a, k)
         sum_into(a, own[a].at[1, 0, 0], ring_q[a].at[2], ring_q[a].at[5])
         mail.post(("Y", a), own[a].at[1, 0, 0], last[a], at.over_y())
+    take_vec(5)
+    vec_out[...] = vec_sum[6]
     for a in range(4):
         mail.take(("Y", a), last[a], at.over_y())
         terms = (own[a].at[0, 0, 0], ring_q[a].at[4], ring_q[a].at[3], last[a])
@@ -720,15 +744,15 @@
     mail.finish()
 
 
-def scatter(lhs, rhs):
+def scatter(lhs, rhs, vec):
     def scratch(*lead):
         return [pltpu.VMEM((*lead, rows, width), bf16) for rows, width in KINDS]
 
     return pl.pallas_call(
         scatter_kernel,
-        out_shape=tuple(jax.ShapeDtypeStruct(kind, f32) for kind in KINDS),
-        in_specs=[ANY] * 8,
-        out_specs=(VMEM,) * 4,
+        out_shape=tuple(jax.ShapeDtypeStruct(kind, f32) for kind in (*KINDS, (16, D))),
+        in_specs=[*[ANY] * 8, VMEM],
+        out_specs=(VMEM,) * 5,
         scratch_shapes=[
             *[pltpu.VMEM((2, 4, 4, rows, 2 * ROWS), bf16) for rows, _ in KINDS],
             *[pltpu.VMEM((2 * ROWS, width), bf16) for _, width in KINDS],
@@ -738,6 +762,8 @@
             *scratch(),
             pltpu.VMEM((128, 2 * ROWS), bf16),
             pltpu.VMEM((512, 2 * ROWS), bf16),
+            pltpu.VMEM((7, 16, D), f32),
+            pltpu.VMEM((6, 16, D), f32),
             pltpu.SemaphoreType.DMA((SCATTER_COPIES,)),
             pltpu.SemaphoreType.DMA((SCATTER_COPIES,)),
             pltpu.SemaphoreType.DMA((8,)),
@@ -746,7 +772,7 @@
             collective_id=2, has_side_effects=True, vmem_limit_bytes=60 * 2**20
         ),
         name="scatter_gradients",
-    )(*lhs, *rhs)
+    )(*lhs, *rhs, vec)
 
 
 def body(
@@ -786,20 +812,20 @@
         ga,
         gb,
     )
-    layer_out, input_grad, n_t, a_t, n2_t, act_t, g_mixed, g_branch, g_up, g_y, g_vec, g_bup = results
+    layer_out, input_grad, n_t, a_t, n2_t, act_t, g_mixed, g_branch, g_up, g_y, g_vec = results
 
     def shards(value, rows):
         return value.reshape(2, 4, 4, 2, rows, ROWS)
 
-    down, up, qkv, out = scatter(
+    down, up, qkv, out, sums = scatter(
         (shards(act_t, 64), shards(n2_t, 16), shards(n_t, 16), shards(a_t, 16)),
         (g_y, g_up, g_mixed, g_branch),
+        g_vec,
     )
-    own_vec = g_vec.reshape(8, 64, 16).transpose(1, 0, 2).reshape(64, 128)
-    both = jnp.concatenate([g_bup[0].reshape(64, 64), own_vec], axis=1)
-    mine = lax.psum_scatter(both, DP, scatter_dimension=0, tiled=True)
-    gbu, rest = mine[:, :64], mine[:, 64:]
-    gv = [rest[:, 16 * k : 16 * k + 16] for k in range(8)]
+    index = lax.axis_index(DP)
+    rest = lax.dynamic_slice(sums, (0, index * 16), (8, 16))
+    gbu = lax.dynamic_slice(sums, (8 + index // 16, index % 16 * 64), (1, 64))
+    gv = [rest[k : k + 1] for k in range(8)]
     return (
         layer_out.reshape(1, 2, BLOCK, D),
         input_grad.reshape(1, 2, BLOCK, D),

time: 627 us -> 296 us (0.47)
  blocking collectives: 330 us -> 0 us
    unnamed x1 -> x0, blocking collectives: 330 us -> none
where the time goes in v2:
time: 296 us
  Pallas kernels  281 us (95%)
  local copies, waits for them, and re-layouts  11.7 us (4%)
    pallas_call x1, Pallas kernels, layer(): pl.pallas_call(layer_kernel_with_bias, out_shape=(out(ROWS, D), out(ROWS,...  117 us
    pallas_call x1, Pallas kernels, scatter(): pl.pallas_call(scatter_kernel, out_shape=tuple((jax.ShapeDtypeStruct(kind...  84.5 us
    pallas_call x1, Pallas kernels, gather(): pl.pallas_call(gather_kernel, out_shape=(jax.ShapeDtypeStruct((2, 4, 4, 2...  79.2 us

profile of v2, /device:TPU:0, one launch (start us, length us, event | category | flops | bytes accessed | tf_op | source)
XLA Modules:
  0.0 295.7 jit_solution(1041738672037602040)
XLA Ops:
  0.6 0.0 copy-start.6
  0.7 0.9 concatenate.6
  1.6 1.7 pad_maximum_fusion.a_ref
  3.3 79.2 %gather_weights.1 = (bf16[2,4,4,2,16,8320]{5,4,3,2,1,0:T(8,128)(2,1)}, bf16[2,4,4,2,64,1024]{5,4,3,2,1,0:T(8,128)(2,1)}) custom-call(bf16[16,8320]{1,0:T(8,128)(2,1)} %pad_maximum_fusion.a_ref, bf16[64,1024]{1,0:T(8,128)(2,1)} %bitcast.38), custom_call_target="tpu_custom_call" | custom-call | tf_op jit(solution)/shard_map/gather_weights/pallas_call | solution.py:205
  82.5 1.0 slice.48
  83.5 0.1 reshape.82
  83.6 0.1 slice.50
  83.7 0.1 copy.40
  83.8 0.1 copy.36
  83.9 0.8 reshape.84.vec
  84.7 0.1 copy.41
  84.8 0.1 copy.37
  84.8 0.1 broadcast_in_dim.19
  84.9 0.7 broadcast_in_dim.20.refs_0_
  85.6 0.0 copy-done.6
  85.6 0.8 copy.38.places
  86.4 0.5 multiply_power_fusion.slopes
  86.9 117.2 %layer.1 = (bf16[256,1024]{1,0:T(8,128)(2,1)}, bf16[256,1024]{1,0:T(8,128)(2,1)}, bf16[1024,256]{1,0:T(8,128)(2,1)}, bf16[1024,256]{1,0:T(8,128)(2,1)}, bf16[102...) custom-call(bf16[256,1024]{1,0:T(8,128)(2,1)} %bitcast.27, ...), custom_call_target="tpu_custom_call" | custom-call | tf_op jit(solution)/shard_map/layer/pallas_call | solution.py:552
  204.1 0.0 copy-start.1
  204.1 0.0 copy-start
  204.2 84.5 %scatter_gradients.1 = (f32[64,1024]{1,0:T(8,128)}, f32[16,4096]{1,0:T(8,128)}, f32[16,3072]{1,0:T(8,128)}, f32[16,1024]{1,0:T(8,128)}, f32[16,1024]{1,0:T(8,128)}) custom-call(bf16[2,4,4,2,64,256]{5,4,3,2,1,0:T(8,128)(2,1)} %bitcast.26, bf16[2,4,4,2,16,256]{5,4,3,2,1,0:T(8,128)(2,1)} %bitcast.31, bf16[2,4,4,2,16,256]{5,4,3,2,1,0:T(8,128)(2,1)} %bitcast.29, ...), custom_call_target="tpu_custom_call" | custom-call | tf_op jit(solution)/shard_map/scatter_gradients/pallas_call | solution.py:751
  288.7 0.0 copy-start.4
  288.7 0.0 copy-start.5
  288.7 0.0 copy-start.3
  288.7 0.0 copy-start.2
  288.7 1.3 dynamic_slice.7
  290.1 0.7 constant_dynamic-slice_fusion
  290.8 0.5 fusion
  291.4 0.0 copy-done.1
  291.4 0.8 copy.48
  292.2 0.0 copy-done
  292.2 0.8 copy.49
  293.0 0.0 copy-done.4
  293.0 0.7 copy.50
  293.6 0.0 copy-done.5
  293.6 0.6 copy.51
  294.3 0.0 copy-done.3
  294.3 0.7 copy.52
  295.0 0.0 copy-done.2
  295.0 0.7 copy.53
  (3 shorter events, 0.0 us)
Async XLA Ops:
  0.6 84.9 %copy-start.6 = (s32[2,128]{1,0:T(2,128)S(1)}, s32[2,128]{1,0:T(2,128)}, u32[]{:S(2)}) copy-start(s32[2,128]{1,0:T(2,128)} %param.17) | copy-start | bytes 3076
  204.1 87.2 %copy-start.1 = (bf16[256,1024]{1,0:T(8,128)(2,1)S(1)}, bf16[256,1024]{1,0:T(8,128)(2,1)}, u32[]{:S(2)}) copy-start(bf16[256,1024]{1,0:T(8,128)(2,1)} %get-tuple-element.35) | copy-start | bytes 1572868
  204.1 88.0 %copy-start = (bf16[256,1024]{1,0:T(8,128)(2,1)S(1)}, bf16[256,1024]{1,0:T(8,128)(2,1)}, u32[]{:S(2)}) copy-start(bf16[256,1024]{1,0:T(8,128)(2,1)} %get-tuple-element.36) | copy-start | bytes 1572868
  288.7 4.3 %copy-start.4 = (f32[16,3072]{1,0:T(8,128)S(1)}, f32[16,3072]{1,0:T(8,128)}, u32[]{:S(2)}) copy-start(f32[16,3072]{1,0:T(8,128)} %get-tuple-element.46) | copy-start | bytes 589828
  288.7 5.0 %copy-start.5 = (f32[16,1024]{1,0:T(8,128)S(1)}, f32[16,1024]{1,0:T(8,128)}, u32[]{:S(2)}) copy-start(f32[16,1024]{1,0:T(8,128)} %get-tuple-element.48) | copy-start | bytes 196612
  288.7 5.6 %copy-start.3 = (f32[16,4096]{1,0:T(8,128)S(1)}, f32[16,4096]{1,0:T(8,128)}, u32[]{:S(2)}) copy-start(f32[16,4096]{1,0:T(8,128)} %get-tuple-element.49) | copy-start | bytes 786436
  288.7 6.3 %copy-start.2 = (f32[64,1024]{1,0:T(8,128)S(1)}, f32[64,1024]{1,0:T(8,128)}, u32[]{:S(2)}) copy-start(f32[64,1024]{1,0:T(8,128)} %get-tuple-element.50) | copy-start | bytes 786436

commit v3 on v1

v3 whole, which is shorter than its diff:
```python
import jax
import jax.numpy as jnp
from jax import lax
from jax.experimental import pallas as pl
from jax.experimental.pallas import tpu as pltpu
from jax.sharding import Mesh
from jax.sharding import PartitionSpec as P

HEADS = 16
D = 1024
FF = 4096
ROWS = 256
BLOCK = 128
QKV0, OUT0, UP0, NA = 128, 3200, 4224, 8320
AXES = ("section", "dp_0", "dp_1", "dp_2", "dp_3")
DP = AXES[1:]
MESH = pl.DeviceIdType.MESH
EPSILON = 1e-05
FAR = 1e30
ANY = pl.BlockSpec(memory_space=pl.ANY)
VMEM = pl.BlockSpec(memory_space=pltpu.VMEM)
SMEM = pl.BlockSpec(memory_space=pltpu.SMEM)
bf16 = jnp.bfloat16
f32 = jnp.float32


class Place:
    def __init__(self):
        self.s, self.yh, self.z, self.x, self.c = [lax.axis_index(a) for a in AXES]
        self.p = jnp.where(self.c == 0, self.z, self.x)
        self.q = jnp.where(self.c == 0, self.x, self.z)

    def zx(self, dp, dq):
        pp, qq = lax.rem(self.p + (dp + 4), 4), lax.rem(self.q + (dq + 4), 4)
        return jnp.where(self.c == 0, pp, qq), jnp.where(self.c == 0, qq, pp)

    def at(self, dp, dq):
        z, x = self.zx(dp, dq)
        return (self.s, self.yh, z, x, self.c)

    def half(self, r):
        return lax.rem(self.yh + r, 2)

    def over_y(self):
        return (self.s, 1 - self.yh, self.z, self.x, self.c)

    def other_core(self):
        return (self.s, self.yh, self.z, self.x, 1 - self.c)

    def neighbours(self):
        return (
            self.over_y(),
            self.other_core(),
            self.at(1, 0),
            self.at(-1, 0),
            self.at(0, 1),
            self.at(0, -1),
        )


def greet(devices):
    barrier = pltpu.get_barrier_semaphore()
    for device in devices:
        pl.semaphore_signal(barrier, inc=1, device_id=device, device_id_type=MESH)
    pl.semaphore_wait(barrier, len(devices))


class Mail:
    def __init__(self, send, recv):
        self.send, self.recv, self.sent, self.number = send, recv, {}, {}

    def post(self, name, src, dst, device):
        self.number.setdefault(name, len(self.number))
        self.sent[name] = (src, dst, device)
        self.copy(name).start()

    def copy(self, name):
        src, dst, device = self.sent[name]
        k = self.number[name]
        return pltpu.make_async_remote_copy(
            src_ref=src() if callable(src) else src,
            dst_ref=dst() if callable(dst) else dst,
            send_sem=self.send.at[k],
            recv_sem=self.recv.at[k],
            device_id=device,
            device_id_type=MESH,
        )

    def take(self, name, dst, device):
        k = self.number[name]
        pltpu.make_async_remote_copy(
            src_ref=dst,
            dst_ref=dst,
            send_sem=self.send.at[k],
            recv_sem=self.recv.at[k],
            device_id=device,
            device_id_type=MESH,
        ).wait_recv()

    def finish(self, names):
        for name in names:
            self.copy(name).wait_send()


def dot(a, b, dims=((1,), (0,))):
    return lax.dot_general(a, b, (dims, ((), ())), preferred_element_type=f32)


NT = ((1,), (1,))
TN = ((0,), (0,))


def cols(j, width, base=0):
    return pl.ds(pl.multiple_of(base + j * width, 128), width)


B_QUERY, B_VALUE, B_OUT, B_DOWN, G_ONE, S_ONE, G_TWO, S_TWO = range(8)
DOWN, UP, QKV, OUT = range(4)
KINDS = ((64, D, None), (16, FF, UP0), (16, 3 * D, QKV0), (16, D, OUT0))
COPIES = 3 * 63 + 4 * (2 + 6 + 6 + 1) + 6 + 2
RING_P, RING_Q, LAST = 32, 56, 62


def step_kernel(
    tokens,
    positions,
    cotangent,
    vec_tile,
    in_qkv,
    in_out,
    in_up,
    in_down,
    layer_out,
    input_grad,
    out_down,
    out_up,
    out_qkv,
    out_out,
    vec_out,
    w1,
    w2,
    xin,
    gyin,
    vec,
    b_up,
    b_qkv,
    xhat1,
    rstd1,
    xhat2,
    rstd2,
    mixed,
    far,
    probs,
    middle,
    gprime,
    act,
    grad,
    act_t,
    n2_t,
    n_t,
    a_t,
    l_down,
    l_up,
    l_qkv,
    l_out,
    r_down,
    r_up,
    r_qkv,
    r_out,
    block,
    block_down,
    vec_sum,
    vec_got,
    send,
    recv,
    load,
    *credits,
):
    at = Place()
    mail = Mail(send, recv)
    section = at.s
    first_section, second_section = section == 0, section == 1
    over_section = (1 - at.s, at.yh, at.z, at.x, at.c)
    my_index = ((at.yh * 4 + at.z) * 4 + at.x) * 2 + at.c
    right_p, left_p, right_q, left_q = at.at(1, 0), at.at(-1, 0), at.at(0, 1), at.at(0, -1)

    def shard_rows(index, rows):
        return pl.ds(pl.multiple_of(index * rows, rows), rows)

    here = shard_rows(my_index, 16)
    placing = [
        pltpu.make_async_copy(vec_tile, w1.at[here, pl.ds(0, 128)], load.at[0]),
        pltpu.make_async_copy(in_qkv, w1.at[here, pl.ds(QKV0, 3 * D)], load.at[1]),
        pltpu.make_async_copy(in_out, w1.at[here, pl.ds(OUT0, D)], load.at[2]),
        pltpu.make_async_copy(in_up, w1.at[here, pl.ds(UP0, FF)], load.at[3]),
        pltpu.make_async_copy(in_down, w2.at[shard_rows(my_index, 64), :], load.at[4]),
    ]
    for copy in placing:
        copy.start()
    greet((*at.neighbours(), over_section))


    def view(t, r, dp, dq, core=None):
        z, x = at.zx(dp, dq)
        index = ((at.half(r) * 4 + z) * 4 + x) * 2 + (at.c if core is None else core)
        if t == 2:
            return w2.at[shard_rows(index, 64), :]
        return w1.at[shard_rows(index, 16), (pl.ds(0, OUT0), pl.ds(OUT0, NA - OUT0))[t]]

    def post(kind, t, r, dp, dq, device):
        v = view(t, r, dp, dq)
        mail.post((kind, t, r, dp, dq), v, v, device)

    def take(kind, t, sent, got):
        mail.take((kind, t, *sent), view(t, *got), right_p)

    def hand_over(t, r, dp, dq):
        post("C", t, r, dp, dq, at.other_core())

    def spread(t, r, dq):
        post("PR", t, r, 0, dq, right_p)
        post("PL", t, r, 0, dq, left_p)
        hand_over(t, r, 0, dq)

    def pass_on(t, dq):
        take("PR", t, (0, 0, dq), (0, -1, dq))
        post("PR2", t, 0, -1, dq, right_p)
        take("PL", t, (1, 0, dq), (1, 1, dq))
        post("PL2", t, 1, 1, dq, left_p)
        hand_over(t, 0, -1, dq)
        hand_over(t, 1, 1, dq)
        take("PL", t, (0, 0, dq), (0, 1, dq))
        take("PR", t, (1, 0, dq), (1, -1, dq))
        hand_over(t, 0, 1, dq)
        hand_over(t, 1, -1, dq)

    def gather_steps(t):
        def s0():
            for copy in {0: placing[:2], 1: placing[2:4], 2: placing[4:]}[t]:
                copy.wait()
            post("Y", t, 0, 0, 0, at.over_y())
            post("QR", t, 0, 0, 0, right_q)
            post("QL", t, 0, 0, 0, left_q)
            spread(t, 0, 0)

        def s1():
            take("Y", t, (0, 0, 0), (1, 0, 0))
            post("QR", t, 1, 0, 0, right_q)
            post("QL", t, 1, 0, 0, left_q)
            spread(t, 1, 0)

        def s2():
            take("QR", t, (0, 0, 0), (0, 0, -1))
            post("QR2", t, 0, 0, -1, right_q)
            spread(t, 0, -1)
            take("QL", t, (0, 0, 0), (0, 0, 1))
            spread(t, 0, 1)

        def s3():
            take("QL", t, (1, 0, 0), (1, 0, 1))
            post("QL2", t, 1, 0, 1, left_q)
            spread(t, 1, 1)
            take("QR", t, (1, 0, 0), (1, 0, -1))
            spread(t, 1, -1)

        def s4():
            pass_on(t, 0)

        def s5():
            take("QR2", t, (0, 0, -1), (0, 0, -2))
            spread(t, 0, 2)
            take("QL2", t, (1, 0, 1), (1, 0, 2))
            spread(t, 1, 2)

        def s9():
            for dq in (0, -1, 1, 2):
                take("PR2", t, (0, -1, dq), (0, -2, dq))
                take("PL2", t, (1, 1, dq), (1, 2, dq))
                hand_over(t, 0, 2, dq)
                hand_over(t, 1, 2, dq)

        def s10():
            for r in range(2):
                for dp in (0, -1, 1, 2):
                    for dq in (0, -1, 1, 2):
                        name = ("C", t, r, dp, dq)
                        mail.take(name, view(t, r, dq, dp, 1 - at.c), at.other_core())

        passing = [lambda dq=dq: pass_on(t, dq) for dq in (-1, 1, 2)]
        return [s0, s1, s2, s3, s4, s5, *passing, s9, s10]


    chunk = 32

    def rows_loop(body):
        @pl.loop(0, ROWS // chunk)
        def _(i):
            body(pl.ds(pl.multiple_of(i * chunk, chunk), chunk))

    g_y, g_branch = r_down.at[pl.ds(0, ROWS), :], r_out.at[pl.ds(0, ROWS), :]
    g_upward, g_mixed = r_up.at[pl.ds(0, ROWS), :], r_qkv.at[pl.ds(0, ROWS), :]
    normed, attended = g_branch, g_y

    row = lax.broadcasted_iota(jnp.int32, (BLOCK, BLOCK), 0)
    col = lax.broadcasted_iota(jnp.int32, (BLOCK, BLOCK), 1)
    low_lane = col < 64

    def make_far():
        distance = col - row
        for b in range(2):
            allowed = (distance >= 0) & (distance <= positions[pl.ds(b, 1), :])
            far[b] = jnp.where(allowed, distance.astype(f32), FAR).T

    def unpack_vectors():
        for j in range(8):
            tiles = [w1[pl.ds((8 * j + i) * 16, 16), pl.ds(0, 128)].astype(f32) for i in range(8)]
            pairs = [tiles[2 * i] + tiles[2 * i + 1] for i in range(4)]
            for i in range(4):
                b_up[:, pl.ds((4 * j + i) * 128, 128)] = pairs[i][8:16]
            vec[:, pl.ds(j * 128, 128)] = ((pairs[0] + pairs[1]) + (pairs[2] + pairs[3]))[0:8]
        b_qkv[pl.ds(0, 1), pl.ds(0, D)] = vec[pl.ds(B_QUERY, 1), :]
        b_qkv[pl.ds(0, 1), pl.ds(D, D)] = jnp.zeros((1, D), f32)
        b_qkv[pl.ds(0, 1), pl.ds(2 * D, D)] = vec[pl.ds(B_VALUE, 1), :]

    def norm_rows(rows, v, xhat, rstd, gain, shift):
        center = v - jnp.mean(v, axis=-1, keepdims=True)
        r = lax.rsqrt(jnp.mean(center * center, axis=-1, keepdims=True) + EPSILON)
        h = center * r
        xhat[rows, :] = h
        rstd[rows, :] = jnp.broadcast_to(r, (chunk, 128))
        return h * vec[pl.ds(gain, 1), :] + vec[pl.ds(shift, 1), :]

    def transpose_into(dst, src):
        @pl.loop(0, D // 256)
        def _(j):
            dst[pl.ds(j * 8, 8)] = src[:, cols(j, 256)].T.reshape(8, 2, 16, ROWS)

    def post_lhs(a):
        mail.post(("L", a), lhs_t[a].at[:, 1 - at.c], lhs_got[a], at.other_core())

    lhs_t, lhs_got = (act_t, n2_t, n_t, a_t), (l_down, l_up, l_qkv, l_out)
    rhs = (r_down, r_up, r_qkv, r_out)

    def norm_one():
        def one(rows):
            v = xin[rows, :].astype(f32)
            normed[rows, :] = norm_rows(rows, v, xhat1, rstd1, G_ONE, S_ONE).astype(bf16)

        rows_loop(one)

    def project(lo, hi):
        @pl.loop(0, hi - lo)
        def _(i):
            j = i + lo
            y = dot(normed[...], w1[:, cols(j, 512, QKV0)])
            mixed[:, cols(j, 512)] = (y + b_qkv[pl.ds(0, 1), cols(j, 512)]).astype(bf16)

    def pair(value):
        zero = jnp.zeros_like(value)
        return jnp.concatenate(
            [jnp.where(low_lane, value, zero), jnp.where(low_lane, zero, value)], axis=0
        )

    def unpair(value):
        return jnp.where(low_lane, value[:BLOCK], value[BLOCK:])

    def slope_rows(hp):
        first = lax.broadcasted_iota(jnp.int32, (2 * BLOCK, 1), 0) < BLOCK
        h = ((2 * hp + 2) - first.astype(jnp.int32)).astype(f32)
        return jnp.exp(h * (-0.5 * 0.6931471805599453))

    def heads(ref, b, part, hp):
        return ref[pl.ds(b * BLOCK, BLOCK), cols(hp, 128, part * D)]

    def attend(lo, hi):
        @pl.loop(0, hi - lo)
        def _(i):
            hp = i + lo
            slope = slope_rows(hp)
            for b in range(2):
                queries = pair(heads(mixed, b, 0, hp))
                scores = dot(queries, heads(mixed, b, 1, hp), NT) * 0.125
                gap = jnp.concatenate([far[b], far[b]], axis=0)
                scores = scores - slope * gap
                e = jnp.exp(scores - jnp.max(scores, axis=-1, keepdims=True))
                p = e * (1.0 / jnp.sum(e, axis=-1, keepdims=True))
                probs[2 * hp + b] = p
                out = unpair(dot(p.astype(bf16), heads(mixed, b, 2, hp)))
                attended[pl.ds(b * BLOCK, BLOCK), cols(hp, 128)] = out.astype(bf16)

    def branch():
        @pl.loop(0, 2)
        def _(j):
            y = dot(attended[...], w1[:, cols(j, 512, OUT0)])
            middle[:, cols(j, 512)] = (
                xin[:, cols(j, 512)].astype(f32) + y + vec[pl.ds(B_OUT, 1), cols(j, 512)]
            )

    def norm_two():
        def two(rows):
            v = middle[rows, :]
            normed[rows, :] = norm_rows(rows, v, xhat2, rstd2, G_TWO, S_TWO).astype(bf16)

        rows_loop(two)

    def rise(lo, hi):
        @pl.loop(0, hi - lo)
        def _(i):
            j = i + lo
            y = dot(normed[...], w1[:, cols(j, 512, UP0)])
            u = y + b_up[pl.ds(0, 1), cols(j, 512)]
            c = 0.7978845608028654
            uu = u * u
            t = jnp.tanh(c * (u + 0.044715 * u * uu))
            half = 0.5 * (1.0 + t)
            a = (u * half).astype(bf16)
            act[:, cols(j, 512)] = a
            act_t[pl.ds(j * 4, 4)] = a.T.reshape(4, 2, 64, ROWS)
            gprime[:, cols(j, 512)] = half + 0.5 * u * (1.0 - t * t) * (
                c * (1.0 + (3 * 0.044715) * uu)
            )

    def first_part():
        def start():
            norm_one()
            transpose_into(n_t, normed)

        def end():
            transpose_into(a_t, attended)

        return [
            start,
            *[lambda j=j: project(2 * j, 2 * j + 2) for j in range(3)],
            *[lambda j=j: attend(2 * j, 2 * j + 2) for j in range(4)],
            end,
        ]

    def second_part():
        def start():
            branch()

        def middle_piece():
            norm_two()
            transpose_into(n2_t, normed)

        return [start, middle_piece, *[lambda j=j: rise(2 * j, 2 * j + 2) for j in range(4)]]

    def weave(steps, pieces):
        done = 0
        for k, step in enumerate(steps):
            step()
            upto = (k + 1) * len(pieces) // len(steps)
            if upto > done:

                @pl.when(first_section)
                def _(todo=tuple(pieces[done:upto])):
                    for piece in todo:
                        piece()

            done = upto

    forth = pltpu.make_async_remote_copy(
        src_ref=layer_out,
        dst_ref=xin,
        send_sem=send.at[COPIES - 2],
        recv_sem=recv.at[COPIES - 2],
        device_id=over_section,
        device_id_type=MESH,
    )
    back = pltpu.make_async_remote_copy(
        src_ref=input_grad,
        dst_ref=gyin,
        send_sem=send.at[COPIES - 1],
        recv_sem=recv.at[COPIES - 1],
        device_id=over_section,
        device_id_type=MESH,
    )

    g0, g1, g2 = gather_steps(0), gather_steps(1), gather_steps(2)
    for step in g0[:6]:
        step()
    make_far()

    @pl.when(first_section)
    def _():
        xin[...] = tokens[...]

    for step in (g1[0], *g0[6:8], g1[1], g0[8], g1[2], g0[9], g1[3], g0[10]):
        step()
    unpack_vectors()
    rest1 = [*g1[4:6], g2[0], g1[6], g2[1], g1[7], g2[2], g1[8], g2[3], g1[9], g1[10]]
    weave(rest1, first_part())
    weave(g2[4:], second_part())

    gathered = list(mail.sent)

    @pl.when(second_section)
    def _():
        mail.finish(gathered)
        forth.wait_recv()
        norm_one()
        transpose_into(n_t, normed)
        project(0, 6)
        attend(0, 8)
        transpose_into(a_t, attended)
        branch()
        norm_two()
        transpose_into(n2_t, normed)
        rise(0, 8)

    for a in (DOWN, UP, QKV, OUT):
        post_lhs(a)

    @pl.loop(0, 2)
    def _(j):
        y = dot(act[...], w2[:, cols(j, 512)])
        y = middle[:, cols(j, 512)] + y + vec[pl.ds(B_DOWN, 1), cols(j, 512)]
        layer_out[:, cols(j, 512)] = y.astype(bf16)

    @pl.when(first_section)
    def _():
        forth.start()
        mail.finish(gathered)
        back.wait_recv()
        g_y[...] = gyin[...]

    @pl.when(second_section)
    def _():
        g_y[...] = cotangent[...]


    def post_rhs(a):
        mine, other = pl.ds(0, ROWS), pl.ds(ROWS, ROWS)
        mail.post(("R", a), rhs[a].at[mine, :], rhs[a].at[other, :], at.other_core())

    sum_neighbours = (right_p, left_p, right_q, left_q, at.over_y())

    def give_room(a):
        for device in sum_neighbours:
            pl.semaphore_signal(credits[a], inc=1, device_id=device, device_id_type=MESH)

    def ready(a):
        mail.take(("L", a), lhs_got[a], at.other_core())
        mail.take(("R", a), rhs[a].at[pl.ds(ROWS, ROWS), :], at.other_core())
        pl.semaphore_wait(credits[a], len(sum_neighbours))

    def room(a, place, count=1):
        rows, width, base = KINDS[a]
        span = pl.ds(place * rows, count * rows)
        return w2.at[span, :] if base is None else w1.at[span, pl.ds(base, width)]

    def own(r, d, e=0):
        return (r * 4 + d) * 4 + e

    def products(a, d):
        rows, width, base = KINDS[a]
        buffer = block_down if rows == 64 else block
        for r in range(2):
            for e in range(4):
                z, x = at.zx(d, e)
                index = (at.half(r) * 4 + z) * 4 + x
                spot = pl.ds((r * 4 + e) * rows, rows)
                buffer[spot, pl.ds(0, ROWS)] = lhs_t[a][index, at.c]
                buffer[spot, pl.ds(ROWS, ROWS)] = lhs_got[a][index]

        @pl.loop(0, width // 512)
        def _(j):
            y = dot(buffer[...], rhs[a][:, cols(j, 512)]).astype(bf16)
            for r in range(2):
                span = pl.ds(own(r, d) * rows, 4 * rows)
                part = y[r * 4 * rows : (r + 1) * 4 * rows]
                if base is None:
                    w2[span, cols(j, 512)] = part
                else:
                    w1[span, cols(j, 512, base)] = part

    def total(a, dst, terms):
        @pl.loop(0, KINDS[a][1] // 512)
        def _(j):
            value = None
            for term in terms:
                piece = term[:, cols(j, 512)].astype(f32)
                value = piece if value is None else value + piece
            dst[:, cols(j, 512)] = value.astype(dst.dtype)

    def sum_p(a, r, d, *ks):
        dst = room(a, own(r, d), 4)
        total(a, dst, (dst, *[room(a, RING_P + 4 * k, 4) for k in ks]))

    def sum_q(a, r, e, *ks):
        dst = room(a, own(r, 0, e))
        total(a, dst, (dst, *[room(a, RING_Q + k) for k in ks]))

    def post_p(a, k, r, d, device):
        src, dst = lambda: room(a, own(r, d), 4), lambda: room(a, RING_P + 4 * k, 4)
        mail.post(("P", a, k), src, dst, device)

    def take_p(a, *ks):
        for k in ks:
            mail.take(("P", a, k), room(a, RING_P + 4 * k, 4), right_p)

    def post_q(a, k, r, e, device):
        mail.post(("Q", a, k), room(a, own(r, 0, e)), room(a, RING_Q + k), device)

    def take_q(a, *ks):
        for k in ks:
            mail.take(("Q", a, k), room(a, RING_Q + k), right_q)

    def a1(a):
        ready(a)
        products(a, 2)
        post_p(a, 0, 0, 2, right_p)
        post_p(a, 1, 1, 2, left_p)

    def a2(a):
        products(a, 1)
        post_p(a, 2, 1, 1, right_p)
        products(a, 3)
        post_p(a, 3, 0, 3, left_p)

    def a3(a):
        take_p(a, 0)
        sum_p(a, 0, 1, 0)
        post_p(a, 4, 0, 1, right_p)
        take_p(a, 1)
        sum_p(a, 1, 3, 1)
        post_p(a, 5, 1, 3, left_p)
        products(a, 0)

    def a4(a):
        take_p(a, 2, 3, 4, 5)
        sum_p(a, 0, 0, 4, 3)
        sum_p(a, 1, 0, 2, 5)
        post_q(a, 0, 0, 2, right_q)
        post_q(a, 1, 1, 2, left_q)
        post_q(a, 2, 1, 1, right_q)
        post_q(a, 3, 0, 3, left_q)

    def a5(a):
        take_q(a, 0)
        sum_q(a, 0, 1, 0)
        post_q(a, 4, 0, 1, right_q)
        take_q(a, 1)
        sum_q(a, 1, 3, 1)
        post_q(a, 5, 1, 3, left_q)

    def a6(a):
        take_q(a, 2, 3, 4, 5)
        sum_q(a, 1, 0, 2, 5)
        mail.post(("Y", a), room(a, own(1, 0)), room(a, LAST), at.over_y())

    outs = (out_down, out_up, out_qkv, out_out)

    def a7(a):
        mail.take(("Y", a), room(a, LAST), right_p)
        terms = (room(a, own(0, 0)), room(a, RING_Q + 4), room(a, RING_Q + 3), room(a, LAST))
        total(a, outs[a], terms)

    def when_first(*steps):
        @pl.when(first_section)
        def _():
            for step, a in steps:
                step(a)

    even_p, even_q = 1 - 2 * lax.rem(at.p, 2), 1 - 2 * lax.rem(at.q, 2)
    partners = (
        at.other_core(),
        at.at(even_p, 0),
        at.at(-even_p, 0),
        at.at(0, even_q),
        at.at(0, -even_q),
        at.over_y(),
    )

    def post_vec(k):
        mail.post(("V", k), vec_sum.at[k], vec_got.at[k], partners[k])

    def take_vec(k):
        mail.take(("V", k), vec_got.at[k], partners[k])
        vec_sum[k + 1] = vec_sum[k] + vec_got[k]


    g_vec = vec_sum.at[0]
    post_rhs(DOWN)
    g_vec[...] = jnp.zeros((16, D), f32)

    @pl.loop(0, 8)
    def _(j):
        g = dot(g_y[...], w2[cols(j, 512), :], NT)
        g = (g * gprime[:, cols(j, 512)]).astype(bf16)
        g_upward[:, cols(j, 512)] = g
        g_vec[pl.ds(8 + j // 2, 1), cols(j % 2, 512)] = jnp.sum(
            g.astype(f32), axis=0, keepdims=True
        )

    post_rhs(UP)
    give_room(DOWN)
    when_first((a1, DOWN))

    @pl.loop(0, 4)
    def _(j):
        grad[:, cols(j, 256)] = dot(g_upward[...], w1[cols(j, 256), pl.ds(UP0, FF)], NT)

    give_room(UP)
    when_first((a2, DOWN))

    def add(index, value):
        g_vec[pl.ds(index, 1), :] = g_vec[pl.ds(index, 1), :] + jnp.sum(
            value, axis=0, keepdims=True
        )

    def norm_back(rows, xhat, rstd, gain, shift):
        dy = grad[rows, :]
        h = xhat[rows, :]
        add(gain, dy * h)
        add(shift, dy)
        dh = dy * vec[pl.ds(gain, 1), :]
        m1 = jnp.mean(dh, axis=-1, keepdims=True)
        m2 = jnp.mean(dh * h, axis=-1, keepdims=True)
        return rstd[rows, pl.ds(0, 1)] * (dh - m1 - h * m2)

    def three(rows):
        gy = g_y[rows, :].astype(f32)
        gm = gy + norm_back(rows, xhat2, rstd2, G_TWO, S_TWO)
        add(B_DOWN, gy)
        middle[rows, :] = gm
        low = gm.astype(bf16)
        g_branch[rows, :] = low
        add(B_OUT, low.astype(f32))

    rows_loop(three)
    post_rhs(OUT)
    when_first((a1, UP))

    @pl.loop(0, 4)
    def _(j):
        y = dot(g_branch[...], w1[cols(j, 256), pl.ds(OUT0, D)], NT)
        act[:, cols(j, 256)] = y.astype(bf16)

    give_room(OUT)

    def attend_back(lo, hi):
        @pl.loop(0, hi - lo)
        def _(i):
            hp = i + lo
            for b in range(2):
                queries = pair(heads(mixed, b, 0, hp))
                keys, values = heads(mixed, b, 1, hp), heads(mixed, b, 2, hp)
                da = pair(heads(act, b, 0, hp))
                p = probs[2 * hp + b]
                dv = dot(p.astype(bf16), da, TN)
                dp = dot(da, values, NT)
                delta = jnp.sum(p * dp, axis=-1, keepdims=True)
                ds = (p * (dp - delta)).astype(bf16)
                dq = unpair(dot(ds, keys)) * 0.125
                dk = dot(ds, queries, TN) * 0.125
                for part, value in enumerate((dq, dk, dv)):
                    span = (pl.ds(b * BLOCK, BLOCK), cols(hp, 128, part * D))
                    g_mixed[span] = value.astype(bf16)

    attend_back(0, 8)
    post_rhs(QKV)
    when_first((a3, DOWN), (a2, UP))

    @pl.loop(0, 4)
    def _(j):
        grad[:, cols(j, 256)] = dot(g_mixed[...], w1[cols(j, 256), pl.ds(QKV0, 3 * D)], NT)

    give_room(QKV)

    def four(rows):
        gx = middle[rows, :] + norm_back(rows, xhat1, rstd1, G_ONE, S_ONE)
        input_grad[rows, :] = gx.astype(bf16)
        add(B_QUERY, g_mixed[rows, pl.ds(0, D)].astype(f32))
        add(B_VALUE, g_mixed[rows, pl.ds(2 * D, D)].astype(f32))

    rows_loop(four)

    @pl.when(second_section)
    def _():
        back.start()
        for step, a in ((a1, DOWN), (a2, DOWN), (a1, UP), (a3, DOWN), (a2, UP)):
            step(a)

    post_vec(0)
    a1(QKV)
    a2(QKV)
    a3(UP)
    take_vec(0)
    post_vec(1)
    a1(OUT)
    a2(OUT)
    a4(DOWN)
    a3(QKV)
    take_vec(1)
    post_vec(2)
    a3(OUT)
    a5(DOWN)
    a4(UP)
    take_vec(2)
    post_vec(3)
    a6(DOWN)
    a5(UP)
    a4(QKV)
    take_vec(3)
    post_vec(4)
    a4(OUT)
    a6(UP)
    a7(DOWN)
    a5(QKV)
    a5(OUT)
    take_vec(4)
    post_vec(5)
    a7(UP)
    a6(QKV)
    a6(OUT)
    take_vec(5)
    vec_out[...] = vec_sum[6]
    a7(QKV)
    a7(OUT)

    @pl.when(first_section)
    def _():
        forth.wait_send()

    @pl.when(second_section)
    def _():
        back.wait_send()

    mail.finish([name for name in mail.sent if name not in gathered])


def step(*args):
    def out(rows, columns, kind=bf16):
        return jax.ShapeDtypeStruct((rows, columns), kind)

    return pl.pallas_call(
        step_kernel,
        out_shape=(
            out(ROWS, D),
            out(ROWS, D),
            *[out(rows, width, f32) for rows, width, _ in KINDS],
            out(16, D, f32),
        ),
        in_specs=[VMEM, VMEM, VMEM, *[ANY] * 5],
        out_specs=(VMEM,) * 7,
        scratch_shapes=[
            pltpu.VMEM((D, NA), bf16),
            pltpu.VMEM((FF, D), bf16),
            pltpu.VMEM((ROWS, D), bf16),
            pltpu.VMEM((ROWS, D), bf16),
            pltpu.VMEM((8, D), f32),
            pltpu.VMEM((8, FF), f32),
            pltpu.VMEM((8, 3 * D), f32),
            pltpu.VMEM((ROWS, D), f32),
            pltpu.VMEM((ROWS, 128), f32),
            pltpu.VMEM((ROWS, D), f32),
            pltpu.VMEM((ROWS, 128), f32),
            pltpu.VMEM((ROWS, 3 * D), bf16),
            pltpu.VMEM((2, BLOCK, BLOCK), f32),
            pltpu.VMEM((16, 2 * BLOCK, BLOCK), f32),
            pltpu.VMEM((ROWS, D), f32),
            pltpu.VMEM((ROWS, FF), f32),
            pltpu.VMEM((ROWS, FF), bf16),
            pltpu.VMEM((ROWS, D), f32),
            *[pltpu.VMEM((32, 2, rows, ROWS), bf16) for rows, _, _ in KINDS],
            *[pltpu.VMEM((32, rows, ROWS), bf16) for rows, _, _ in KINDS],
            *[pltpu.VMEM((2 * ROWS, width), bf16) for _, width, _ in KINDS],
            pltpu.VMEM((128, 2 * ROWS), bf16),
            pltpu.VMEM((512, 2 * ROWS), bf16),
            pltpu.VMEM((7, 16, D), f32),
            pltpu.VMEM((6, 16, D), f32),
            pltpu.SemaphoreType.DMA((COPIES,)),
            pltpu.SemaphoreType.DMA((COPIES,)),
            pltpu.SemaphoreType.DMA((5,)),
            *[pltpu.SemaphoreType.REGULAR] * 4,
        ],
        compiler_params=pltpu.CompilerParams(
            collective_id=0, has_side_effects=True, vmem_limit_bytes=62 * 2**20
        ),
        name="step",
    )(*args)


def lay_out_kernel(index, *refs):
    big_in, sums, big_out, vectors = refs[:6], refs[6], refs[7:13], refs[13:]
    for src, dst in zip(big_in, big_out):
        dst[...] = src[...]
    i = index[0]
    own = sums[pl.ds(0, 8), cols(i // 8, 128)]
    own = pltpu.roll(own, lax.rem(128 - lax.rem(i, 8) * 16, 128), 1)
    for k in range(8):
        vectors[k][...] = own[k : k + 1, 0:16]
    rows = sums[pl.ds(8, 8), cols(lax.rem(i, 16) // 2, 128)]
    rows = pltpu.roll(rows, lax.rem(128 - lax.rem(i, 2) * 64, 128), 1)
    row = lax.broadcasted_iota(jnp.int32, (8, 128), 0) == i // 16
    vectors[8][...] = jnp.sum(jnp.where(row, rows, 0.0), axis=0, keepdims=True)[:, 0:64]


def lay_out(index, big, sums):
    return pl.pallas_call(
        lay_out_kernel,
        out_shape=(
            *[jax.ShapeDtypeStruct(v.shape, v.dtype) for v in big],
            *[jax.ShapeDtypeStruct((1, 16), f32)] * 8,
            jax.ShapeDtypeStruct((1, 64), f32),
        ),
        in_specs=[SMEM, *[VMEM] * 7],
        out_specs=(VMEM,) * 15,
        compiler_params=pltpu.CompilerParams(vmem_limit_bytes=32 * 2**20),
        name="lay_out",
    )(index, *big, sums)


def body(
    tokens,
    positions,
    cotangent,
    w_qkv,
    b_query,
    b_value,
    w_out,
    b_out,
    w_up,
    b_up,
    w_down,
    b_down,
    gain_one,
    shift_one,
    gain_two,
    shift_two,
):
    index = lax.axis_index(DP)
    small = (b_query, b_value, b_out, b_down, gain_one, shift_one, gain_two, shift_two)
    lane = jnp.arange(128)[None]
    rows = jnp.tile(jnp.concatenate(small, axis=0), (1, 8))
    rows = jnp.where(lane // 16 == index % 8, rows, jnp.zeros_like(rows))
    wide = jnp.tile(b_up, (8, 2))
    wide = jnp.where(lane // 64 == index % 2, wide, jnp.zeros_like(wide))
    *big, sums = step(
        tokens.reshape(ROWS, D),
        positions,
        cotangent.reshape(ROWS, D),
        jnp.concatenate([rows, wide], axis=0),
        w_qkv[0],
        w_out[0],
        w_up[0],
        w_down[0],
    )
    layer_out, input_grad, down, up, qkv, out, *vectors = lay_out(
        jnp.reshape(index, (1,)).astype(jnp.int32), big, sums
    )
    return (
        layer_out.reshape(1, 2, BLOCK, D),
        input_grad.reshape(1, 2, BLOCK, D),
        qkv[None],
        vectors[B_QUERY],
        vectors[B_VALUE],
        out[None],
        vectors[B_OUT],
        up[None],
        vectors[8],
        down[None],
        vectors[B_DOWN],
        vectors[G_ONE],
        vectors[S_ONE],
        vectors[G_TWO],
        vectors[S_TWO],
    )


def solution(mesh):
    torus = Mesh(mesh.devices.reshape(2, 2, 4, 4, 2), AXES)
    rows, matrix, vector = P(None, DP, None), P("section", DP, None), P("section", DP)
    of_layer = P("section", None, DP, None)
    return jax.shard_map(
        body,
        mesh=torus,
        in_specs=(
            rows,
            P(None, DP),
            rows,
            matrix,
            vector,
            vector,
            matrix,
            vector,
            matrix,
            vector,
            matrix,
            vector,
            vector,
            vector,
            vector,
            vector,
        ),
        out_specs=(
            of_layer,
            of_layer,
            matrix,
            vector,
            vector,
            matrix,
            vector,
            matrix,
            vector,
            matrix,
            vector,
            vector,
            vector,
            vector,
            vector,
        ),
        check_vma=False,
    )
```

time: 627 us -> 253 us (0.40)
  blocking collectives: 330 us -> 0 us
  Pallas kernels: 276 us -> 243 us
  local copies, waits for them, and re-layouts: 17.8 us -> 8.07 us
    unnamed x1 -> x0, blocking collectives: 330 us -> none
    pallas_call x3 -> x2, Pallas kernels: 276 us -> 243 us  [the longest x1 242 us: step(): pl.pallas_call(step_kernel, out_shape=(out(ROWS, D), out(ROWS, D), *[out(...]
where the time goes in v3:
time: 253 us
  Pallas kernels  243 us (96%)
  local copies, waits for them, and re-layouts  8.07 us (3%)
    pallas_call x1, Pallas kernels, step(): pl.pallas_call(step_kernel, out_shape=(out(ROWS, D), out(ROWS, D), *[out(...  242 us
    unnamed x32, local copies, waits for them, and re-layouts  7.84 us

profile of v3, /device:TPU:0, one launch (start us, length us, event | category | flops | bytes accessed | tf_op | source)
XLA Modules:
  0.0 252.7 jit_solution(6002619425252413569)
XLA Ops:
  0.7 0.0 copy-start.15
  0.7 0.0 copy-start.14
  0.7 0.6 copy-done.15
  1.4 0.0 copy-start.10
  1.4 0.0 copy-start.11
  1.4 0.0 copy-start.12
  1.4 0.0 copy-start.13
  1.4 0.0 copy-start.7
  1.4 0.0 copy-start.8
  1.4 0.0 copy-start.9
  1.4 0.1 tile.26
  1.5 0.0 copy-done.14
  1.5 0.5 copy-done.10
  2.0 0.0 copy-done.11
  2.0 0.0 copy-done.12
  2.0 0.0 copy-done.13
  2.1 0.0 copy-done.7
  2.1 0.0 copy-done.8
  2.1 0.0 copy-done.9
  2.1 0.1 tile.23
  2.2 0.6 pad_maximum_fusion.vec_tile
  2.8 241.8 %step.1 = (bf16[256,1024]{1,0:T(8,128)(2,1)}, bf16[256,1024]{1,0:T(8,128)(2,1)}, f32[64,1024]{1,0:T(8,128)}, f32[16,4096]{1,0:T(8,128)}, f32[16,3072]{1,0:T(8,12...) custom-call(bf16[256,1024]{1,0:T(8,128)(2,1)} %bitcast.14, s32[2,128]{1,0:T(2,128)} %positions.1, bf16[256,1024]{1,0:T(8,128)(2,1)} %bitcast.15, ...), custom_call_target="tpu_custom_call" | custom-call | tf_op jit(solution)/shard_map/step/pallas_call | solution.py:837
  244.7 0.0 copy-start
  244.7 1.0 copy-done
  245.7 0.0 copy-start.1
  245.7 1.0 copy-done.1
  246.8 0.0 copy-start.2
  246.8 0.9 copy-done.2
  247.7 0.0 copy-start.3
  247.7 0.9 copy-done.3
  248.7 0.0 copy-start.4
  248.7 0.9 copy-done.4
  249.6 0.0 copy-start.5
  249.6 0.8 copy-done.5
  250.5 0.0 copy-start.6
  250.5 0.8 copy-done.6
  251.3 1.3 lay_out.1
  (6 shorter events, 0.1 us)
Async XLA Ops:
  0.7 0.7 copy-start.15
  0.7 0.8 copy-start.14
  1.4 0.7 copy-start.10
  1.4 0.7 copy-start.11
  1.4 0.7 copy-start.12
  1.4 0.7 copy-start.13
  1.4 0.7 copy-start.7
  1.4 0.7 copy-start.8
  1.4 0.7 copy-start.9
  244.7 1.0 copy-start
  245.7 1.0 copy-start.1
  246.8 0.9 copy-start.2
  247.7 0.9 copy-start.3
  248.7 0.9 copy-start.4
  249.6 0.8 copy-start.5
  250.5 0.8 copy-start.6
